TPU v7x, 32 devices: a whole 2x2x4 slice. The times are simulated.
32 devices in a mesh: leaf: 32 (over z, y, x, core).
Axes of the slice: x: 2, y: 2, z: 4, core: 2. Of those that a mesh axis runs over, the one named last changes fastest.
Arguments:
- points: float32 [16, 65536], P(None, 'leaf'), may hold values from -6 to 6
- order: int32 [65536], P('leaf'), may hold values from 0 to 65535, as said below
- bases: float32 [256, 256, 64], P('leaf'), may hold values from -0.375 to 0.375
- lift: float32 [256, 64, 64], P('leaf'), may hold values from -0.25 to 0.25
- near_ids: int32 [256, 3], P('leaf'), may hold values from 0 to 255, as said below
- near_blocks: float32 [256, 3, 256, 256], P('leaf'), may hold values from -0.21875 to 0.21875
- far_ids: int32 [256, 8], P('leaf'), may hold values from 0 to 255, as said below
- far_count: int32 [256], P('leaf'), may hold values from 1 to 8
- far_blocks: float32 [256, 8, 64, 64], P('leaf'), may hold values from -0.25 to 0.25
- transfer: float32 [4, 2, 64, 64], replicated, may hold values from -0.5 to 0.5
- couple: float32 [4, 4, 64, 64], replicated, may hold values from -0.375 to 0.375
- links: int32 [32, 4, 4], P('leaf'), may hold values from 0 to 1, as said below
- top_couple: float32 [64, 64], replicated, may hold values from -0.75 to 0.75
Outputs:
- product: float32 [16, 65536], P(None, 'leaf')
Inputs may be any that keep to these rules, and one draw needn't show every extreme that they name: `order`: each subtree's 2048 entries are a permutation of that subtree's positions. `near_ids`: the first entry of a leaf is the leaf itself; the others lie at most one leaf away. `far_ids`: a coupled leaf lies in a subtree at most 4 subtrees away from the leaf's own; slots at or beyond far_count are padding. links[d, l, k] is the same for all d in one aligned block of 2^l subtrees.
All inputs are finite; a program needn't handle non-finite values.
Results may differ from a plain program's by a relative error of at most 0.0001.
Values sent between devices are 32-bit elements; how exact they have to be, the bound alone decides.
No kernel may reach another device: no remote copies, remote signals or barrier semaphores. Data moves between devices by JAX's collectives and lax.ppermute only.
A program may use at most 64 MiB of HBM per device.

v0:
```python
import jax
import jax.numpy as jnp
from jax import lax
from jax.sharding import PartitionSpec as P

REACH = 4
DEPTH = 4


HIGHEST_PRECISION = lax.Precision.HIGHEST
OFFSETS = (-3, -2, 2, 3)


def extended_2(block, sides, width):
    for axis, dim in sides:
        count = lax.axis_size(axis)
        forward = [(i, i + 1) for i in range(count - 1)]
        backward = [(target, source) for source, target in forward]
        low = lax.ppermute(
            lax.slice_in_dim(block, block.shape[dim] - width, None, axis=dim), axis, forward
        )
        high = lax.ppermute(lax.slice_in_dim(block, 0, width, axis=dim), axis, backward)
        block = jnp.concatenate([low, block, high], axis=dim)
    return block


def from_behind(x, axis, by):
    count = lax.axis_size(axis)
    pairs = [(i, i + by) for i in range(count) if 0 <= i + by < count]
    return lax.ppermute(x, axis, pairs)


def full_tree(node_zero, link_table, transfer, couple, top_couple):
    levels = [node_zero]
    for level in range(DEPTH):
        current = levels[-1]
        paired = current.reshape(current.shape[0] // 2, 2, current.shape[1], current.shape[2])
        parent = jnp.einsum(
            "rq,nrs->nqs", transfer[level, 0], paired[:, 0], precision=HIGHEST_PRECISION
        )
        parent = parent + jnp.einsum(
            "rq,nrs->nqs", transfer[level, 1], paired[:, 1], precision=HIGHEST_PRECISION
        )
        levels.append(parent)
    couplings = []
    for level in range(DEPTH):
        current = levels[level]
        node_count = current.shape[0]
        chosen_links = link_table[:: 1 << level, level, :].astype(jnp.float32)
        padded = jnp.pad(current, ((3, 3), (0, 0), (0, 0)))
        summed = jnp.zeros_like(current)
        for column, offset in enumerate(OFFSETS):
            partner = padded[3 + offset : 3 + offset + node_count]
            term = jnp.einsum(
                "qr,nrs->nqs", couple[level, column], partner, precision=HIGHEST_PRECISION
            )
            summed = summed + chosen_links[:, column][:, None, None] * term
        couplings.append(summed)
    top_nodes = levels[DEPTH]
    top_count = top_nodes.shape[0]
    spots = jnp.arange(top_count, dtype=jnp.int32)
    distance = jnp.abs(spots[:, None] - spots[None, :])
    weight = jnp.where(distance >= 2, 1.0 / jnp.maximum(distance, 1).astype(jnp.float32), 0.0)
    blended = jnp.einsum("nm,mrs->nrs", weight, top_nodes, precision=HIGHEST_PRECISION)
    downward = jnp.einsum("qr,nrs->nqs", top_couple, blended, precision=HIGHEST_PRECISION)
    for level in reversed(range(DEPTH)):
        even_part = jnp.einsum(
            "rq,nqs->nrs", transfer[level, 0], downward, precision=HIGHEST_PRECISION
        )
        odd_part = jnp.einsum(
            "rq,nqs->nrs", transfer[level, 1], downward, precision=HIGHEST_PRECISION
        )
        spread = jnp.stack([even_part, odd_part], axis=1).reshape(
            -1, downward.shape[1], downward.shape[2]
        )
        downward = couplings[level] + spread
    return downward


def local(
    points,
    order,
    bases,
    lift,
    near_ids,
    near_blocks,
    far_ids,
    far_count,
    far_blocks,
    transfer,
    couple,
    links,
    top_couple,
):
    position = lax.axis_index("leaf")
    vectors, points_dev = points.shape
    leaf_dev, leaf_size, rank_size = bases.shape
    local_order = order - position * points_dev
    tree_x = jnp.take(points, local_order, axis=1)
    blocks = tree_x.reshape(vectors, leaf_dev, leaf_size)
    leaf_coef = jnp.einsum("lpr,slp->lrs", bases, blocks, precision=HIGHEST_PRECISION)
    node_zero = jnp.einsum("lrq,lrs->qs", lift, leaf_coef, precision=HIGHEST_PRECISION)
    extended = extended_2(tree_x, (("leaf", 1),), leaf_size)
    extended = extended.reshape(vectors, leaf_dev + 2, leaf_size)
    near_local = near_ids - position * leaf_dev + 1
    gathered = jnp.take(extended, near_local, axis=1)
    near_part = jnp.einsum("lkpq,slkq->slp", near_blocks, gathered, precision=HIGHEST_PRECISION)
    pieces = []
    for offset in range(-REACH, REACH + 1):
        if offset == 0:
            pieces.append(leaf_coef)
        else:
            pieces.append(from_behind(leaf_coef, "leaf", -offset))
    window = jnp.stack(pieces).reshape((2 * REACH + 1) * leaf_dev, rank_size, vectors)
    window_slot = (far_ids // leaf_dev - position + REACH) * leaf_dev + far_ids % leaf_dev
    picked = jnp.take(window, window_slot, axis=0)
    active = (jnp.arange(far_ids.shape[1], dtype=jnp.int32)[None, :] < far_count[:, None]).astype(
        jnp.float32
    )
    picked = picked * active[:, :, None, None]
    far_part = jnp.einsum("lkrq,lkqs->lrs", far_blocks, picked, precision=HIGHEST_PRECISION)
    all_nodes, all_links = (
        lax.all_gather(node_zero[None], "leaf", axis=0, tiled=True),
        lax.all_gather(links, "leaf", axis=0, tiled=True),
    )
    down_all = full_tree(all_nodes, all_links, transfer, couple, top_couple)
    down_zero = lax.dynamic_index_in_dim(down_all, position, 0, keepdims=False)
    leaf_out = jnp.einsum("lrq,qs->lrs", lift, down_zero, precision=HIGHEST_PRECISION) + far_part
    tree_y = near_part + jnp.einsum("lpr,lrs->slp", bases, leaf_out, precision=HIGHEST_PRECISION)
    tree_y = tree_y.reshape(vectors, points_dev)
    return jnp.zeros((vectors, points_dev), jnp.float32).at[:, local_order].set(tree_y)


def solution(mesh):
    in_specs = (
        P(None, "leaf"),
        P("leaf"),
        P("leaf", None, None),
        P("leaf", None, None),
        P("leaf", None),
        P("leaf", None, None, None),
        P("leaf", None),
        P("leaf"),
        P("leaf", None, None, None),
        P(),
        P(),
        P("leaf", None, None),
        P(),
    )
    out_specs = P(None, "leaf")
    return jax.shard_map(local, mesh=mesh, in_specs=in_specs, out_specs=out_specs, check_vma=False)
```

profile of v0, /device:TPU:0, one launch (start us, length us, event | category | flops | bytes accessed | tf_op | source)
XLA Modules:
  0.0 181.4 jit_solution(7877075720154721448)
XLA Ops:
  0.0 0.9 compare_and_fusion
  1.5 2.2 %copy.119 = f32[16,2048]{0,1:T(8,128)} copy(f32[16,2048]{1,0:T(8,128)} %param.13) | data formatting | bytes 262144 | tf_op args[0]
  3.7 6.7 %gather_fusion = f32[2048,16]{1,0:T(8,128)S(1)} fusion(f32[16,2048]{0,1:T(8,128)} %copy.119, s32[2048]{0:T(1024)S(1)} %broadcast_clamp_fusion), kind=kCustom, calls=%fused_computation | custom fusion | bytes 270336 | tf_op jit(solution)/shard_map/jit(_take)/gather | solution.py:99
  10.7 1.6 fusion.38
  12.3 5.6 %collective-permute-start.2 = (f32[8,64,16]{1,2,0:T(8,128)S(1)}, f32[8,64,16]{1,2,0:T(8,128)}, u32[]{:S(2)}, u32[]{:S(2)}) collective-permute-start(f32[8,64,16]{1,2,0:T(8,128)S(1)} %bitcast.393), channel_id=1, source_target_pairs={{0,4},{1,5},{2,6},{3,7},{4,8},{5,9},{6,10},{7,11},{8,12},{9,13},{1... | collective-permute-start | bytes 98312 | tf_op jit(solution)/shard_map/ppermute | solution.py:30
  18.0 3.2 %collective-permute-start.3 = (f32[8,64,16]{1,2,0:T(8,128)S(1)}, f32[8,64,16]{1,2,0:T(8,128)}, u32[]{:S(2)}, u32[]{:S(2)}) collective-permute-start(f32[8,64,16]{1,2,0:T(8,128)S(1)} %bitcast.394), channel_id=1, source_target_pairs={{0,3},{1,4},{2,5},{3,6},{4,7},{5,8},{6,9},{7,10},{8,11},{9,12},{10... | collective-permute-start | bytes 98312 | tf_op jit(solution)/shard_map/ppermute | solution.py:30
  21.1 3.4 %collective-permute-start.4 = (f32[8,64,16]{1,2,0:T(8,128)S(1)}, f32[8,64,16]{1,2,0:T(8,128)}, u32[]{:S(2)}, u32[]{:S(2)}) collective-permute-start(f32[8,64,16]{1,2,0:T(8,128)S(1)} %bitcast.395), channel_id=1, source_target_pairs={{0,2},{1,3},{2,4},{3,5},{4,6},{5,7},{6,8},{7,9},{8,10},{9,11},{10,... | collective-permute-start | bytes 98312 | tf_op jit(solution)/shard_map/ppermute | solution.py:30
  24.5 1.6 bitcast_select_fusion
  26.1 0.7 fusion.152
  26.8 2.7 %collective-permute-start = (f32[16,256]{0,1:T(8,128)}, f32[16,256]{0,1:T(8,128)}, u32[]{:S(2)}, u32[]{:S(2)}) collective-permute-start(f32[16,256]{0,1:T(8,128)} %get-tuple-element.15), channel_id=1, source_target_pairs={{0,1},{1,2},{2,3},{3,4},{4,5},{5,6},{6,7},{7,8},{8,9},{9,10},{10,1... | collective-permute-start | bytes 49160 | tf_op jit(solution)/shard_map/ppermute | solution.py:19
  29.5 1.3 collective-permute-start.1
  30.8 38.4 %all_gather.6 = s32[32,4,4]{2,1,0:T(4,128)S(1)} all-gather(s32[1,4,4]{2,1,0:T(4,128)S(1)} %copy-done.8), channel_id=1, replica_groups=mesh['leaf'=32] {'leaf'}, dimensions={0}, use_global_device_ids=true | all-gather | bytes 2112 | tf_op jit(solution)/shard_map/all_gather | solution.py:124
  69.2 1.2 convolution_bitcast_fusion.12
  70.4 37.3 %all-gather.1 = f32[32,64,16]{1,2,0:T(8,128)S(1)} all-gather(f32[1,64,16]{1,2,0:T(8,128)S(1)} %convolution_bitcast_fusion.12), channel_id=2, replica_groups=mesh['leaf'=32] {'leaf'}, dimensions={0}, use_global_device_ids=true | all-gather | bytes 135168 | tf_op jit(solution)/shard_map/all_gather | solution.py:123
  107.8 1.0 fusion.33
  111.1 0.9 convolution_multiply_fusion.15
  112.0 0.9 fusion.20
  113.0 0.9 fusion.19
  114.0 0.9 fusion.18
  114.9 0.8 convolution_bitcast_fusion.7
  115.7 0.8 convolution_bitcast_fusion.8
  116.6 1.0 convolution_multiply_fusion.11
  117.6 0.8 pad_maximum_fusion.3
  118.3 1.0 fusion.14
  119.3 1.0 fusion.13
  120.3 1.0 fusion.12
  121.3 1.0 convolution_bitcast_fusion.4
  122.3 1.0 convolution_bitcast_fusion.5
  123.3 0.7 copy.142
  124.0 1.0 convolution_multiply_fusion.4
  125.0 1.0 convolution_multiply_fusion.5
  126.1 1.0 convolution_multiply_fusion.6
  127.1 1.2 fusion.9
  128.3 1.0 convolution_bitcast_fusion.1
  129.3 1.0 convolution_bitcast_fusion.2
  130.4 1.0 copy.127
  131.5 0.9 copy.143
  132.4 0.8 compare_and_fusion.1
  133.3 0.7 compare_and_fusion.2
  134.2 1.1 convolution_multiply_fusion.3
  135.3 1.1 fusion.3
  136.4 1.1 fusion.2
  137.6 1.8 %fusion.1 = f32[32,64,16]{1,0,2:T(8,128)} fusion(f32[32,16,64]{2,0,1:T(8,128)S(1)} %fusion.2, f32[32,64,16]{1,0,2:T(8,128)S(1)} %copy.127, f32[32]{0:T(128)S(1)} %get-tuple-element.17, f32[4,4,64,64]{3,2,1,0:T(8,128)} %param.23), kind=kOutput, calls=%fused_computation.6 | convolution fusion | flops 25231360 | bytes 426112 | tf_op jit(solution)/shard_map/qr,nrs->nqs/dot_general | solution.py:54
  139.4 0.9 dynamic-slice_add_fusion
  140.7 2.3 %collective-permute-start.5 = (f32[8,64,16]{1,2,0:T(8,128)S(1)}, f32[8,64,16]{1,2,0:T(8,128)S(1)}, u32[]{:S(2)}, u32[]{:S(2)}) collective-permute-start(f32[8,64,16]{1,2,0:T(8,128)S(1)} %bitcast.396), channel_id=1, source_target_pairs={{0,1},{1,2},{2,3},{3,4},{4,5},{5,6},{6,7},{7,8},{8,9},{9,10},{10,1... | collective-permute-start | bytes 98312 | tf_op jit(solution)/shard_map/ppermute | solution.py:30
  143.0 1.0 copy.120
  143.9 1.3 collective-permute-start.6
  145.2 1.0 copy.122
  146.8 7.3 %convolution_bitcast_fusion = f32[8,16,256]{2,1,0:T(8,128)S(1)} fusion(f32[8,3,256,256]{3,2,1,0:T(8,128)} %param.18, f32[8,3,16,256]{3,2,1,0:T(8,128)S(1)} %bitcast.389, pred[8,3]{1,0:T(8,128)(4,1)S(1)} %copy.118), kind=kOutput, calls=%fused_computation.14 | convolution fusion | flops 302088192 | bytes 6815768 | tf_op jit(solution)/shard_map/lkpq,slkq->slp/dot_general | solution.py:107
  154.2 1.3 collective-permute-start.7
  155.5 0.8 bitcast_dynamic-update-slice_fusion.8
  156.3 1.3 collective-permute-start.8
  157.6 0.8 bitcast_dynamic-update-slice_fusion.7
  158.4 1.5 collective-permute-start.9
  159.9 0.8 bitcast_dynamic-update-slice_fusion.6
  160.8 1.3 collective-permute-done.7
  162.1 2.1 %collective-permute-done.8 = f32[8,64,16]{1,2,0:T(8,128)S(1)} collective-permute-done((f32[8,64,16]{1,2,0:T(8,128)S(1)}, f32[8,64,16]{1,2,0:T(8,128)S(1)}, u32[]{:S(2)}, u32[]{:S(2)}) %collective-permute-start.8) | collective-permute-done | bytes 32800 | tf_op jit(solution)/shard_map/ppermute | solution.py:30
  164.2 4.9 %collective-permute-done.9 = f32[8,64,16]{1,2,0:T(8,128)S(1)} collective-permute-done((f32[8,64,16]{1,2,0:T(8,128)S(1)}, f32[8,64,16]{1,2,0:T(8,128)S(1)}, u32[]{:S(2)}, u32[]{:S(2)}) %collective-permute-start.9) | collective-permute-done | bytes 32800 | tf_op jit(solution)/shard_map/ppermute | solution.py:30
  169.1 0.6 gather_fusion.2
  169.8 1.9 %convolution_bitcast_fusion.6 = f32[8,64,16]{1,2,0:T(8,128)S(1)} fusion(f32[8,8,64,64]{3,2,1,0:T(8,128)S(1)} %copy-done, f32[8,8,64,16]{2,3,1,0:T(8,128)S(1)} %bitcast.379, f32[8,8]{1,0:T(8,128)S(1)} %get-tuple-element.29, pred[8,8]{1,0:T(8,128)(4,1)S(1)} %get-tuple-element.9), kind=kOutput, calls=%fused_computation.41 | convolution fusion | flops 50462720 | bytes 1343808 | tf_op jit(solution)/shard_map/lkrq,lkqs->lrs/dot_general | solution.py:121
  171.7 0.7 fusion.15
  172.9 1.3 copy.145
  174.2 6.2 %scatter_custom_fusion = f32[16,2048]{0,1:T(8,128)S(1)} fusion(s32[2048]{0:T(1024)} %copy-done.6, f32[2048,16]{1,0:T(8,128)} %copy.145, f32[]{:T(128)} %constant.62.clone.1), kind=kCustom, calls=%fused_computation.63 | custom fusion | bytes 131584 | tf_op jit(solution)/shard_map/scatter | solution.py:131
  180.4 1.0 copy.146
  (76 shorter events, 5.2 us)
Async XLA Ops:
  0.0 169.8 %copy-start = (f32[8,8,64,64]{3,2,1,0:T(8,128)S(1)}, f32[8,8,64,64]{3,2,1,0:T(8,128)}, u32[]{:S(2)}) copy-start(f32[8,8,64,64]{3,2,1,0:T(8,128)} %param.21) | copy-start | bytes 3145732
  0.9 0.6 copy-start.6
  10.4 10.8 %copy-start.1 = (f32[2048,16]{1,0:T(8,128)}, f32[2048,16]{1,0:T(8,128)S(1)}, u32[]{:S(2)}) copy-start(f32[2048,16]{1,0:T(8,128)S(1)} %gather_fusion) | copy-start | bytes 393220
  10.4 20.4 %copy-start.8 = (s32[1,4,4]{2,1,0:T(4,128)S(1)}, s32[1,4,4]{2,1,0:T(4,128)}, u32[]{:S(2)}) copy-start(s32[1,4,4]{2,1,0:T(4,128)} %param.24) | copy-start | bytes 196
  10.7 98.1 %copy-start.4 = (f32[4,2,64,64]{3,2,1,0:T(8,128)S(1)}, f32[4,2,64,64]{3,2,1,0:T(8,128)}, u32[]{:S(2)}) copy-start(f32[4,2,64,64]{3,2,1,0:T(8,128)} %param.22) | copy-start | bytes 393220
  12.3 98.0 %copy-start.7 = (f32[64,64]{1,0:T(8,128)S(1)}, f32[64,64]{1,0:T(8,128)}, u32[]{:S(2)}) copy-start(f32[64,64]{1,0:T(8,128)} %param.25) | copy-start | bytes 49156
  12.3 141.8 %collective-permute-start.2 = (f32[8,64,16]{1,2,0:T(8,128)S(1)}, f32[8,64,16]{1,2,0:T(8,128)}, u32[]{:S(2)}, u32[]{:S(2)}) collective-permute-start(f32[8,64,16]{1,2,0:T(8,128)S(1)} %bitcast.393), channel_id=1, source_target_pairs={{0,4},{1,5},{2,6},{3,7},{4,8},{5,9},{6,10},{7,11},{8,12},{9,13},{1... | collective-permute-start | bytes 98312 | tf_op jit(solution)/shard_map/ppermute | solution.py:30
  18.0 138.3 %collective-permute-start.3 = (f32[8,64,16]{1,2,0:T(8,128)S(1)}, f32[8,64,16]{1,2,0:T(8,128)}, u32[]{:S(2)}, u32[]{:S(2)}) collective-permute-start(f32[8,64,16]{1,2,0:T(8,128)S(1)} %bitcast.394), channel_id=1, source_target_pairs={{0,3},{1,4},{2,5},{3,6},{4,7},{5,8},{6,9},{7,10},{8,11},{9,12},{10... | collective-permute-start | bytes 98312 | tf_op jit(solution)/shard_map/ppermute | solution.py:30
  21.1 137.3 %collective-permute-start.4 = (f32[8,64,16]{1,2,0:T(8,128)S(1)}, f32[8,64,16]{1,2,0:T(8,128)}, u32[]{:S(2)}, u32[]{:S(2)}) collective-permute-start(f32[8,64,16]{1,2,0:T(8,128)S(1)} %bitcast.395), channel_id=1, source_target_pairs={{0,2},{1,3},{2,4},{3,5},{4,6},{5,7},{6,8},{7,9},{8,10},{9,11},{10,... | collective-permute-start | bytes 98312 | tf_op jit(solution)/shard_map/ppermute | solution.py:30
  26.8 113.9 %collective-permute-start = (f32[16,256]{0,1:T(8,128)}, f32[16,256]{0,1:T(8,128)}, u32[]{:S(2)}, u32[]{:S(2)}) collective-permute-start(f32[16,256]{0,1:T(8,128)} %get-tuple-element.15), channel_id=1, source_target_pairs={{0,1},{1,2},{2,3},{3,4},{4,5},{5,6},{6,7},{7,8},{8,9},{9,10},{10,1... | collective-permute-start | bytes 49160 | tf_op jit(solution)/shard_map/ppermute | solution.py:19
  29.5 114.4 %collective-permute-start.1 = (f32[16,256]{0,1:T(8,128)}, f32[16,256]{0,1:T(8,128)}, u32[]{:S(2)}, u32[]{:S(2)}) collective-permute-start(f32[16,256]{0,1:T(8,128)} %get-tuple-element.16), channel_id=1, source_target_pairs={{1,0},{2,1},{3,2},{4,3},{5,4},{6,5},{7,6},{8,7},{9,8},{10,9},{11,1... | collective-permute-start | bytes 49160 | tf_op jit(solution)/shard_map/ppermute | solution.py:22
  107.8 1.0 copy-start.2
  140.7 20.1 %collective-permute-start.5 = (f32[8,64,16]{1,2,0:T(8,128)S(1)}, f32[8,64,16]{1,2,0:T(8,128)S(1)}, u32[]{:S(2)}, u32[]{:S(2)}) collective-permute-start(f32[8,64,16]{1,2,0:T(8,128)S(1)} %bitcast.396), channel_id=1, source_target_pairs={{0,1},{1,2},{2,3},{3,4},{4,5},{5,6},{6,7},{7,8},{8,9},{9,10},{10,1... | collective-permute-start | bytes 98312 | tf_op jit(solution)/shard_map/ppermute | solution.py:30
  143.9 16.9 %collective-permute-start.6 = (f32[8,64,16]{1,2,0:T(8,128)S(1)}, f32[8,64,16]{1,2,0:T(8,128)S(1)}, u32[]{:S(2)}, u32[]{:S(2)}) collective-permute-start(f32[8,64,16]{1,2,0:T(8,128)S(1)} %bitcast.397), channel_id=1, source_target_pairs={{1,0},{2,1},{3,2},{4,3},{5,4},{6,5},{7,6},{8,7},{9,8},{10,9},{11,1... | collective-permute-start | bytes 98312 | tf_op jit(solution)/shard_map/ppermute | solution.py:30
  154.2 8.0 %collective-permute-start.7 = (f32[8,64,16]{1,2,0:T(8,128)S(1)}, f32[8,64,16]{1,2,0:T(8,128)S(1)}, u32[]{:S(2)}, u32[]{:S(2)}) collective-permute-start(f32[8,64,16]{1,2,0:T(8,128)S(1)} %bitcast.398), channel_id=1, source_target_pairs={{2,0},{3,1},{4,2},{5,3},{6,4},{7,5},{8,6},{9,7},{10,8},{11,9},{12,... | collective-permute-start | bytes 98312 | tf_op jit(solution)/shard_map/ppermute | solution.py:30
  156.3 7.9 %collective-permute-start.8 = (f32[8,64,16]{1,2,0:T(8,128)S(1)}, f32[8,64,16]{1,2,0:T(8,128)S(1)}, u32[]{:S(2)}, u32[]{:S(2)}) collective-permute-start(f32[8,64,16]{1,2,0:T(8,128)S(1)} %bitcast.399), channel_id=1, source_target_pairs={{3,0},{4,1},{5,2},{6,3},{7,4},{8,5},{9,6},{10,7},{11,8},{12,9},{13... | collective-permute-start | bytes 98312 | tf_op jit(solution)/shard_map/ppermute | solution.py:30
  158.4 10.7 %collective-permute-start.9 = (f32[8,64,16]{1,2,0:T(8,128)S(1)}, f32[8,64,16]{1,2,0:T(8,128)S(1)}, u32[]{:S(2)}, u32[]{:S(2)}) collective-permute-start(f32[8,64,16]{1,2,0:T(8,128)S(1)} %bitcast.400), channel_id=1, source_target_pairs={{4,0},{5,1},{6,2},{7,3},{8,4},{9,5},{10,6},{11,7},{12,8},{13,9},{1... | collective-permute-start | bytes 98312 | tf_op jit(solution)/shard_map/ppermute | solution.py:30
  169.8 2.0 %copy-start.5 = (f32[8,64,64]{2,1,0:T(8,128)S(1)}, f32[8,64,64]{2,1,0:T(8,128)}, u32[]{:S(2)}) copy-start(f32[8,64,64]{2,1,0:T(8,128)} %param.16) | copy-start | bytes 393220
  169.8 2.7 %copy-start.3 = (f32[8,256,64]{1,2,0:T(8,128)S(1)}, f32[8,256,64]{1,2,0:T(8,128)}, u32[]{:S(2)}) copy-start(f32[8,256,64]{1,2,0:T(8,128)} %param.15) | copy-start | bytes 1572868
where the time goes:
time: 184 us; the launch traced here: 181 us
  blocking collectives  75.7 us (41%)
  matrix products  38.8 us (21%)
  local copies, waits for them, and re-layouts  28.5 us (15%)
  starting transfers between devices  23.8 us (13%)
  waiting for transfers between devices  8.32 us (5%)
  other arithmetic  5.64 us (3%)
    all_gather x1, blocking collectives, local(): lax.all_gather(links, 'leaf', axis=0, tiled=True)  38.4 us
    all_gather x1, blocking collectives, local(): lax.all_gather(node_zero[None], 'leaf', axis=0, tiled=True)  37.3 us
    ppermute x8, starting transfers between devices, from_behind(): return lax.ppermute(x, axis, pairs)  19.8 us
    dot_general x16, matrix products, full_tree(): jnp.einsum('qr,nrs->nqs', couple[level, column], partner, precision=HIGHE...  17.1 us
    ppermute x8, waiting for transfers between devices, from_behind(): return lax.ppermute(x, axis, pairs)  8.32 us
    dot_general x1, matrix products, local(): jnp.einsum('lkpq,slkq->slp', near_blocks, gathered, precision=HIGHEST_PRE...  7.31 us
    scatter x2, local copies, waits for them, and re-layouts, local(): jnp.zeros((vectors, points_dev), jnp.float32).at[:, local_order].set(tree_y)  7.17 us
    gather x2, local copies, waits for them, and re-layouts, local(): tree_x = jnp.take(points, local_order, axis=1)  6.98 us
  transfers between devices with their start and end apart: 10, of which 3 were waited for; matrix products, arithmetic and copies ran while one was open for 27% of the time, Pallas kernels for 0%

commit v1 on v0

v1 whole, which is shorter than its diff:
```python
import functools

import jax
import jax.numpy as jnp
from jax import lax
from jax.experimental import pallas as pl
from jax.experimental.pallas import tpu as pltpu
from jax.sharding import PartitionSpec as P

REACH = 4
DEPTH = 4
OFFSETS = (-3, -2, 2, 3)
GROUP = 2 * REACH
LANES = 128
VMEM_LIMIT = 48 * 1024 * 1024

NN = (((1,), (0,)), ((), ()))
NT = (((1,), (1,)), ((), ()))

VMEM = pl.BlockSpec(memory_space=pltpu.VMEM)
SMEM = pl.BlockSpec(memory_space=pltpu.SMEM)


def halves(x):
    high = x.astype(jnp.bfloat16)
    low = (x - high.astype(jnp.float32)).astype(jnp.bfloat16)
    return high, low


def dot3(a, b, dims):
    a_high, a_low = halves(a)
    b_high, b_low = halves(b)
    rows = a.shape[0]
    both = lax.dot_general(
        jnp.concatenate([a_high, a_low], axis=0), b_high, dims, preferred_element_type=jnp.float32
    )
    cross = lax.dot_general(a_high, b_low, dims, preferred_element_type=jnp.float32)
    return both[:rows] + (both[rows:] + cross)


def fold(x):
    return jnp.concatenate([x[:8], x[8:]], axis=1)


def beside(p, q):
    rank = p.shape[1] // 2
    left = lax.broadcasted_iota(jnp.int32, p.shape, 1) < rank
    return jnp.concatenate(
        [
            jnp.where(left, p, pltpu.roll(q, rank, 1)),
            jnp.where(left, pltpu.roll(p, rank, 1), q),
        ],
        axis=0,
    )


def lane_gather(x, high, low):
    rows, columns = x.shape
    high = jnp.broadcast_to(high, (rows, LANES))
    low = jnp.broadcast_to(low, (rows, LANES))
    result = jnp.zeros((rows, LANES), x.dtype)
    for source in range(columns // LANES):
        tile = x[:, source * LANES : (source + 1) * LANES]
        moved = jnp.take_along_axis(tile, low, axis=1, mode="promise_in_bounds")
        result = jnp.where(high == source, moved, result)
    return result


def up_kernel(me_ref, points_ref, order_ref, bases_ref, lift_ref, near_out, wide_out, node_out, x_out):
    me = me_ref[0]
    leaf_dev, rank, leaf_size = bases_ref.shape
    vectors, points_dev = points_ref.shape
    tiles = points_dev // LANES
    points = points_ref[...]
    base = me * points_dev
    for t in range(tiles):
        spot = order_ref[t : t + 1, :] - base
        x_out[:, t * LANES : (t + 1) * LANES] = lane_gather(
            points, lax.shift_right_logical(spot, 7), spot & (LANES - 1)
        )
    coefs = []
    for leaf in range(leaf_dev):
        x_leaf = x_out[:, leaf * leaf_size : (leaf + 1) * leaf_size]
        coefs.append(dot3(x_leaf, bases_ref[leaf], NT))
    for leaf in range(leaf_dev):
        tile = fold(coefs[leaf])
        for peer in range(GROUP):
            near_out[peer, leaf * 8 : (leaf + 1) * 8, :] = tile
            wide_out[peer, leaf * 8 : (leaf + 1) * 8, :] = tile
    node = dot3(jnp.concatenate(coefs, axis=1), lift_ref[...].reshape(leaf_dev * rank, rank), NN)
    tile = fold(node)
    for peer in range(node_out.shape[0]):
        node_out[peer] = tile
    top = leaf_dev * 8
    half = leaf_size // LANES
    for out, place in ((near_out, lax.rem(me, GROUP)), (wide_out, lax.rem(me + REACH, GROUP))):
        for peer in range(GROUP):
            for part in range(half):
                first = x_out[:, part * LANES : (part + 1) * LANES]
                start = points_dev - leaf_size + part * LANES
                last = x_out[:, start : start + LANES]
                out[peer, top + part * vectors : top + (part + 1) * vectors, :] = jnp.where(
                    place < peer, last, first
                )


def inverse_kernel(me_ref, order_ref, inverse_out):
    points_dev = order_ref.shape[1]
    tiles = points_dev // LANES
    spot = order_ref[...] - me_ref[0] * points_dev
    high = lax.shift_right_logical(spot, 7)
    low = spot & (LANES - 1)
    times = lax.broadcasted_iota(jnp.int32, (1, points_dev), 1)
    shape = (tiles, points_dev)
    match = lax.broadcasted_iota(jnp.int32, shape, 0) == jnp.broadcast_to(high, shape)
    coarse = lax.shift_right_logical(times, 4).astype(jnp.float32)
    fine = (times & 15).astype(jnp.float32)
    left = jnp.concatenate(
        [
            jnp.where(match, jnp.broadcast_to(coarse, shape), 0.0),
            jnp.where(match, jnp.broadcast_to(fine, shape), 0.0),
        ],
        axis=0,
    ).astype(jnp.bfloat16)
    shape = (LANES, points_dev)
    right = jnp.where(
        lax.broadcasted_iota(jnp.int32, shape, 0) == jnp.broadcast_to(low, shape), 1.0, 0.0
    ).astype(jnp.bfloat16)
    both = lax.dot_general(left, right, NT, preferred_element_type=jnp.float32)
    inverse_out[...] = (both[:tiles] * 16.0 + both[tiles:]).astype(jnp.int32)


def near_kernel(me_ref, ids_ref, x_ref, blocks_ref, out_ref):
    leaf = pl.program_id(0)
    _, slots, leaf_size, _ = blocks_ref.shape
    leaf_dev = pl.num_programs(0)
    first = me_ref[0] * leaf_dev
    total = jnp.zeros(out_ref.shape[1:], jnp.float32)
    for slot in range(slots):
        local = ids_ref[leaf, slot] - first
        here = (local >= 0) & (local < leaf_dev)
        x_leaf = x_ref[jnp.clip(local, 0, leaf_dev - 1)]
        x_leaf = jnp.where(here, x_leaf, 0.0)
        total = total + dot3(x_leaf, blocks_ref[0, slot], NT)
    out_ref[0] = total


def down_kernel(
    me_ref,
    near_ids_ref,
    far_ids_ref,
    far_count_ref,
    links_ref,
    near_in,
    wide_in,
    nodes_in,
    near_part,
    inverse_ref,
    bases_ref,
    lift_ref,
    first_ref,
    last_ref,
    far_ref,
    transfer_ref,
    couple_ref,
    top_ref,
    out_ref,
    window,
    edges,
    y_tree,
    *levels,
):
    me = me_ref[0]
    leaf_dev, rank, leaf_size = bases_ref.shape
    slots = far_ids_ref.shape[1]
    vectors, points_dev = out_ref.shape
    count = nodes_in.shape[0]
    coef_rows = leaf_dev * 8
    parts = leaf_size // LANES
    place = lax.rem(me, GROUP)
    place_wide = lax.rem(me + REACH, GROUP)

    for index in range(2 * REACH + 1):
        offset = index - REACH
        inside = (place + offset >= 0) & (place + offset < GROUP)
        narrow = near_in[jnp.clip(place + offset, 0, GROUP - 1), :coef_rows]
        wide = wide_in[jnp.clip(place_wide + offset, 0, GROUP - 1), :coef_rows]
        window[index * leaf_dev : (index + 1) * leaf_dev] = jnp.where(inside, narrow, wide).reshape(
            leaf_dev, 8, LANES
        )
    window[(2 * REACH + 1) * leaf_dev] = jnp.zeros((8, LANES), jnp.float32)
    for index, offset in ((0, -1), (1, 1)):
        inside = (place + offset >= 0) & (place + offset < GROUP)
        narrow = near_in[jnp.clip(place + offset, 0, GROUP - 1), coef_rows:]
        wide = wide_in[jnp.clip(place_wide + offset, 0, GROUP - 1), coef_rows:]
        chosen = jnp.where(inside, narrow, wide)
        edges[index] = jnp.concatenate(
            [chosen[part * vectors : (part + 1) * vectors] for part in range(parts)], axis=1
        )

    for level in range(DEPTH):
        half = count >> (level + 1)
        source = nodes_in if level == 0 else levels[level - 1]
        pairs = [beside(source[2 * n], source[2 * n + 1]) for n in range(half)]
        weights = transfer_ref[level].reshape(2 * rank, rank)
        parents = dot3(jnp.concatenate(pairs, axis=0), weights, NN)
        for n in range(half):
            levels[level][n] = fold(parents[n * vectors : (n + 1) * vectors])

    top_count = count >> DEPTH
    node = lax.shift_right_logical(me, DEPTH)
    blended = jnp.zeros((8, LANES), jnp.float32)
    for other in range(top_count):
        distance = jnp.abs(node - other)
        weight = jnp.where(
            distance >= 2, 1.0 / jnp.maximum(distance, 1).astype(jnp.float32), 0.0
        )
        blended = blended + weight * levels[DEPTH - 1][other]
    down = dot3(beside(blended, blended)[:, :rank], top_ref[...], NT)
    for level in reversed(range(DEPTH)):
        node = lax.shift_right_logical(me, level)
        size = count >> level
        source = nodes_in if level == 0 else levels[level - 1]
        partners = []
        for column, offset in enumerate(OFFSETS):
            other = node + offset
            used = (other >= 0) & (other < size)
            weight = jnp.where(used, links_ref[level, column], 0).astype(jnp.float32)
            partners.append(weight * source[jnp.clip(other, 0, size - 1)])
        left = jnp.concatenate(
            [beside(partners[0], partners[1]), beside(partners[2], partners[3])], axis=1
        )
        weights = jnp.concatenate([couple_ref[level, column] for column in range(4)], axis=1)
        out = dot3(left, weights, NT)
        down = out + dot3(down, transfer_ref[level, lax.rem(node, 2)], NT)

    zero_slot = (2 * REACH + 1) * leaf_dev
    for leaf in range(leaf_dev):
        picked = []
        for slot in range(slots):
            spot = far_ids_ref[leaf, slot] - (me - REACH) * leaf_dev
            used = (slot < far_count_ref[leaf]) & (spot >= 0) & (spot < zero_slot)
            picked.append(window[jnp.where(used, spot, zero_slot)])
        left = jnp.concatenate(
            [beside(picked[slot], picked[slot + 1]) for slot in range(0, slots, 2)] + [down], axis=1
        )
        weights = jnp.concatenate(
            [far_ref[leaf, slot] for slot in range(slots)] + [lift_ref[leaf]], axis=1
        )
        leaf_out = dot3(left, weights, NT)
        y_leaf = near_part[leaf] + dot3(leaf_out, bases_ref[leaf], NN)
        y_tree[:, leaf * leaf_size : (leaf + 1) * leaf_size] = y_leaf
    for leaf, outside, index, blocks in (
        (0, -1, 0, first_ref),
        (leaf_dev - 1, leaf_dev, 1, last_ref),
    ):
        total = jnp.zeros((vectors, leaf_size), jnp.float32)
        for slot in range(1, blocks.shape[1]):
            remote = near_ids_ref[leaf, slot] - me * leaf_dev == outside
            total = total + dot3(jnp.where(remote, edges[index], 0.0), blocks[0, slot], NT)
        start = leaf * leaf_size
        y_tree[:, start : start + leaf_size] = y_tree[:, start : start + leaf_size] + total

    y = y_tree[...]
    for tile in range(points_dev // LANES):
        spot = inverse_ref[tile : tile + 1, :]
        out_ref[:, tile * LANES : (tile + 1) * LANES] = lane_gather(
            y, lax.shift_right_logical(spot, 7), spot & (LANES - 1)
        )


def local(
    devices,
    points,
    order,
    bases,
    lift,
    near_ids,
    near_blocks,
    far_ids,
    far_count,
    far_blocks,
    transfer,
    couple,
    links,
    top_couple,
):
    me = lax.axis_index("leaf").astype(jnp.int32).reshape(1)
    vectors, points_dev = points.shape
    leaf_dev, leaf_size, rank = bases.shape
    slots = near_ids.shape[1]
    bases_t = jnp.swapaxes(bases, 1, 2)
    tiles = points_dev // LANES
    rows = leaf_dev * 8 + vectors * (leaf_size // LANES)
    params = pltpu.CompilerParams(vmem_limit_bytes=VMEM_LIMIT)
    f32 = jnp.float32

    near_out, wide_out, node_out, tree_x = pl.pallas_call(
        up_kernel,
        out_shape=[
            jax.ShapeDtypeStruct((GROUP, rows, LANES), f32),
            jax.ShapeDtypeStruct((GROUP, rows, LANES), f32),
            jax.ShapeDtypeStruct((devices, 8, LANES), f32),
            jax.ShapeDtypeStruct((vectors, points_dev), f32),
        ],
        in_specs=[SMEM] + [VMEM] * 4,
        out_specs=[VMEM] * 4,
        compiler_params=params,
        name="up",
    )(me, points, order.reshape(tiles, LANES), bases_t, lift)

    narrow_groups = [[g * GROUP + i for i in range(GROUP)] for g in range(devices // GROUP)]
    wide_groups = [
        [(g * GROUP - REACH + i) % devices for i in range(GROUP)] for g in range(devices // GROUP)
    ]
    nodes_in = lax.all_to_all(node_out, "leaf", 0, 0, tiled=True)
    near_in = lax.all_to_all(near_out, "leaf", 0, 0, axis_index_groups=narrow_groups, tiled=True)
    wide_in = lax.all_to_all(wide_out, "leaf", 0, 0, axis_index_groups=wide_groups, tiled=True)

    inverse = pl.pallas_call(
        inverse_kernel,
        out_shape=jax.ShapeDtypeStruct((tiles, LANES), jnp.int32),
        in_specs=[SMEM, VMEM],
        out_specs=VMEM,
        compiler_params=params,
        name="inverse",
    )(me, order.reshape(1, points_dev))

    x_leaves = tree_x.reshape(vectors, leaf_dev, leaf_size).swapaxes(0, 1)
    near_part = pl.pallas_call(
        near_kernel,
        grid=(leaf_dev,),
        out_shape=jax.ShapeDtypeStruct((leaf_dev, vectors, leaf_size), f32),
        in_specs=[
            SMEM,
            SMEM,
            pl.BlockSpec((leaf_dev, vectors, leaf_size), lambda i: (0, 0, 0)),
            pl.BlockSpec((1, slots, leaf_size, leaf_size), lambda i: (i, 0, 0, 0)),
        ],
        out_specs=pl.BlockSpec((1, vectors, leaf_size), lambda i: (i, 0, 0)),
        compiler_params=params,
        cost_estimate=pl.CostEstimate(
            flops=6 * vectors * near_blocks.size, bytes_accessed=4 * near_blocks.size, transcendentals=0
        ),
        name="near",
    )(me, near_ids, x_leaves, near_blocks)

    def edge(block):
        return pl.BlockSpec((1, slots, leaf_size, leaf_size), lambda i: (block, 0, 0, 0))

    def whole(shape):
        return pl.BlockSpec(shape, lambda i: (0,) * len(shape))

    operands = (near_in, wide_in, nodes_in, near_part, inverse, bases_t, lift)
    after = (far_blocks, transfer, couple, top_couple)
    return pl.pallas_call(
        down_kernel,
        grid=(1,),
        out_shape=jax.ShapeDtypeStruct((vectors, points_dev), f32),
        in_specs=[SMEM] * 5
        + [whole(x.shape) for x in operands]
        + [edge(0), edge(leaf_dev - 1)]
        + [whole(x.shape) for x in after],
        out_specs=whole((vectors, points_dev)),
        scratch_shapes=[
            pltpu.VMEM(((2 * REACH + 1) * leaf_dev + 1, 8, LANES), f32),
            pltpu.VMEM((2, vectors, leaf_size), f32),
            pltpu.VMEM((vectors, points_dev), f32),
        ]
        + [pltpu.VMEM((devices >> (level + 1), 8, LANES), f32) for level in range(DEPTH)],
        compiler_params=params,
        name="down",
    )(
        me,
        near_ids,
        far_ids,
        far_count,
        links.reshape(links.shape[1:]),
        *operands,
        near_blocks,
        near_blocks,
        *after,
    )


def solution(mesh):
    in_specs = (
        P(None, "leaf"),
        P("leaf"),
        P("leaf", None, None),
        P("leaf", None, None),
        P("leaf", None),
        P("leaf", None, None, None),
        P("leaf", None),
        P("leaf"),
        P("leaf", None, None, None),
        P(),
        P(),
        P("leaf", None, None),
        P(),
    )
    return jax.shard_map(
        functools.partial(local, mesh.shape["leaf"]),
        mesh=mesh,
        in_specs=in_specs,
        out_specs=P(None, "leaf"),
        check_vma=False,
    )
```

time: 184 us -> 59.8 us (0.33)
  blocking collectives: 75.7 us -> 26.2 us
  matrix products: 38.8 us -> 0 us
  starting transfers between devices: 23.8 us -> 6 us
  local copies, waits for them, and re-layouts: 28.5 us -> 12.6 us
  Pallas kernels: 0 us -> 14.1 us
  waiting for transfers between devices: 8.32 us -> 0.01 us
  other arithmetic: 5.64 us -> 0 us
    all_gather x2 -> x0, blocking collectives: 75.7 us -> none  [the longest x1 38.4 us: local(): lax.all_gather(links, 'leaf', axis=0, tiled=True)]
    dot_general x40 -> x0, matrix products: 38.8 us -> none  [the longest x16 17.1 us: full_tree(): jnp.einsum('qr,nrs->nqs', couple[level, column], partner, precision=HIGHE...]
    all_to_all x0 -> x2, blocking collectives: none -> 26.2 us  [the longest x1 15.4 us: local(): nodes_in = lax.all_to_all(node_out, 'leaf', 0, 0, tiled=True)]
    ppermute x10 -> x0, starting transfers between devices: 23.8 us -> none  [the longest x8 19.8 us: from_behind(): return lax.ppermute(x, axis, pairs)]
    pallas_call x0 -> x4, Pallas kernels: none -> 14.1 us  [the longest x1 6.37 us: local(): pl.pallas_call(near_kernel, grid=(leaf_dev,), out_shape=jax.ShapeDtypeStr...]
    ppermute x10 -> x0, waiting for transfers between devices: 8.32 us -> none  [the longest x8 8.32 us: from_behind(): return lax.ppermute(x, axis, pairs)]
    gather x4 -> x0, local copies, waits for them, and re-layouts: 8.18 us -> none  [the longest x2 6.98 us: local(): tree_x = jnp.take(points, local_order, axis=1)]
    scatter x2 -> x0, local copies, waits for them, and re-layouts: 7.17 us -> none  [local(): jnp.zeros((vectors, points_dev), jnp.float32).at[:, local_order].set(tree_y)]
  transfers between devices with their start and end apart: 10 -> 1, of which waited for: 3 -> 0; matrix products, arithmetic and copies ran while one was open for 27% -> 2% of each run, Pallas kernels for 0% -> 11%
where the time goes in v1:
time: 59.8 us; the launch traced here: 59 us
  blocking collectives  26.2 us (44%)
  Pallas kernels  14.1 us (24%)
  local copies, waits for them, and re-layouts  12.6 us (21%)
  starting transfers between devices  6 us (10%)
    all_to_all x1, blocking collectives, local(): nodes_in = lax.all_to_all(node_out, 'leaf', 0, 0, tiled=True)  15.4 us
    unnamed x35, local copies, waits for them, and re-layouts  11.9 us
    all_to_all x1, blocking collectives, local(): lax.all_to_all(near_out, 'leaf', 0, 0, axis_index_groups=narrow_groups, t...  10.7 us
    pallas_call x1, Pallas kernels, local(): pl.pallas_call(near_kernel, grid=(leaf_dev,), out_shape=jax.ShapeDtypeStr...  6.37 us
    pallas_call x1, Pallas kernels, local(): pl.pallas_call(down_kernel, grid=(1,), out_shape=jax.ShapeDtypeStruct((ve...  6.23 us
    all_to_all x1, starting transfers between devices, local(): lax.all_to_all(wide_out, 'leaf', 0, 0, axis_index_groups=wide_groups, til...  6 us
    pallas_call x1, Pallas kernels, local(): pl.pallas_call(up_kernel, out_shape=[jax.ShapeDtypeStruct((GROUP, rows, L...  1.26 us
  transfers between devices with their start and end apart: 1, of which 0 were waited for; matrix products, arithmetic and copies ran while one was open for 2% of the time, Pallas kernels for 11%

profile of v1, /device:TPU:0, one launch (start us, length us, event | category | flops | bytes accessed | tf_op | source)
XLA Modules:
  0.0 59.0 jit_solution(15450198106976134152)
XLA Ops:
  0.0 0.0 copy-start.14
  0.0 0.0 copy-start
  0.0 1.1 %copy-done = f32[8,256,64]{1,2,0:T(8,128)S(1)} copy-done((f32[8,256,64]{1,2,0:T(8,128)S(1)}, f32[8,256,64]{1,2,0:T(8,128)}, u32[]{:S(2)}) %copy-start) | copy-done | bytes 524312
  1.1 0.0 copy-start.3
  1.1 0.9 %copy-done.3 = f32[8,64,64]{2,1,0:T(8,128)S(1)} copy-done((f32[8,64,64]{2,1,0:T(8,128)S(1)}, f32[8,64,64]{2,1,0:T(8,128)}, u32[]{:S(2)}) %copy-start.3) | copy-done | bytes 131096
  2.0 0.0 copy-start.10
  2.0 0.9 %copy-done.10 = f32[16,2048]{1,0:T(8,128)S(1)} copy-done((f32[16,2048]{1,0:T(8,128)S(1)}, f32[16,2048]{1,0:T(8,128)}, u32[]{:S(2)}) %copy-start.10) | copy-done | bytes 131096
  2.9 0.0 copy-start.12
  2.9 0.7 %copy-done.12 = s32[2048]{0:T(1024)S(1)} copy-done((s32[2048]{0:T(1024)S(1)}, s32[2048]{0:T(1024)}, u32[]{:S(2)}) %copy-start.12) | copy-done | bytes 8216
  3.6 0.0 copy-start.1
  3.6 0.0 copy-start.2
  3.6 1.3 %up.1 = (f32[8,96,128]{2,1,0:T(8,128)S(1)}, f32[8,96,128]{2,1,0:T(8,128)S(1)}, f32[32,8,128]{2,1,0:T(8,128)S(1)}, f32[16,2048]{1,0:T(8,128)S(1)}) custom-call(s32[1]{0:T(128)} %bitcast.me_ref, f32[16,2048]{1,0:T(8,128)S(1)} %copy-done.10, s32[16,128]{1,0:T(8,128)S(1)} %bitcast.16, f32[8,64,256]{2,1,0:T(8,128)S(1)} %bitcast.12, f32[8,64,64]{2,1,0:T(8,128)S(1)} %copy-done.3), custom_call_target="tpu_custom_call" | custom-call | tf_op jit(solution)/shard_map/up/pallas_call | solution.py:298
  4.9 0.0 copy-start.8
  4.9 15.4 %all_to_all.15.nodes_in = f32[32,8,128]{2,1,0:T(8,128)} all-to-all(f32[32,8,128]{2,1,0:T(8,128)S(1)} %get-tuple-element.11), channel_id=1, replica_groups=mesh['leaf'=32] {'leaf'}, dimensions={0} | all-to-all | bytes 262144 | tf_op jit(solution)/shard_map/all_to_all | solution.py:316
  20.3 10.7 %all_to_all.16.near_in = f32[8,96,128]{2,1,0:T(8,128)S(1)} all-to-all(f32[8,96,128]{2,1,0:T(8,128)S(1)} %get-tuple-element.9), channel_id=1, replica_groups={{0,1,2,3,4,5,6,7},{8,9,10,11,12,13,14,15},{16,17,18,19,20,21,22,23},{24..., dimensions={0} | all-to-all | bytes 786432 | tf_op jit(solution)/shard_map/all_to_all | solution.py:317
  31.1 0.0 copy-done.8
  31.1 6.0 %all-to-all-start.1 = ((f32[8,96,128]{2,1,0:T(8,128)}), f32[8,96,128]{2,1,0:T(8,128)S(1)}, u32[]{:S(2)}, u32[]{:S(2)}) async-start(f32[8,96,128]{2,1,0:T(8,128)} %copy-done.8), calls=%async_computation.1 | async-start | bytes 786432 | tf_op jit(solution)/shard_map/all_to_all | solution.py:318
  37.1 0.7 %copy.21 = f32[2,8,8,256]{3,2,0,1:T(8,128)} copy(f32[2,8,8,256]{3,2,1,0:T(8,128)S(1)} %bitcast.15) | data formatting | bytes 262144 | tf_op jit(solution)/shard_map/reshape | solution.py:329
  37.7 0.8 %copy.18.ids_ref.near_ids_ref = s32[8,3]{1,0:T(8,128)S(1)} copy(s32[8,3]{0,1:T(4,128)} %param.17) | data formatting | bytes 192 | tf_op args[4]
  38.5 0.0 copy-start.13
  38.5 0.7 %copy-done.13 = s32[2048]{0:T(1024)S(1)} copy-done((s32[2048]{0:T(1024)S(1)}, s32[2048]{0:T(1024)}, u32[]{:S(2)}) %copy-start.13) | copy-done | bytes 8216
  39.2 0.3 inverse.1.inverse_ref
  39.5 0.0 copy-start.7
  39.5 0.9 %copy-done.7 = f32[2,8,8,256]{3,2,0,1:T(8,128)S(1)} copy-done((f32[2,8,8,256]{3,2,0,1:T(8,128)S(1)}, f32[2,8,8,256]{3,2,0,1:T(8,128)}, u32[]{:S(2)}) %copy-start.7) | copy-done | bytes 131096
  40.4 6.4 %near.1.near_part = f32[8,16,256]{2,1,0:T(8,128)S(1)} custom-call(s32[1]{0:T(128)} %bitcast.me_ref, s32[8,3]{1,0:T(8,128)S(1)} %copy.18.ids_ref.near_ids_ref, f32[8,16,256]{2,1,0:T(8,128)S(1)} %bitcast.14, f32[8,3,256,256]{3,2,1,0:T(8,128)} %last_ref.1), custom_call_target="tpu_custom_call" | custom-call | flops 150994944 | bytes 6291456 | tf_op jit(solution)/shard_map/near/pallas_call | solution.py:330
  46.7 0.0 all-to-all-done.1.wide_in
  46.8 0.0 copy-done.14
  46.8 0.0 copy-done.1
  46.8 0.0 copy-done.2
  46.8 0.0 copy-start.4
  46.8 0.9 %copy-done.4 = f32[8,64,64]{2,1,0:T(8,128)S(1)} copy-done((f32[8,64,64]{2,1,0:T(8,128)S(1)}, f32[8,64,64]{2,1,0:T(8,128)}, u32[]{:S(2)}) %copy-start.4) | copy-done | bytes 131096
  47.7 0.0 copy-start.5
  47.7 0.9 %copy-done.5 = f32[32,8,128]{2,1,0:T(8,128)S(1)} copy-done((f32[32,8,128]{2,1,0:T(8,128)S(1)}, f32[32,8,128]{2,1,0:T(8,128)}, u32[]{:S(2)}) %copy-start.5) | copy-done | bytes 131096
  48.6 0.0 copy-start.6
  48.6 1.0 %copy-done.6 = f32[4,4,64,64]{3,2,1,0:T(8,128)S(1)} copy-done((f32[4,4,64,64]{3,2,1,0:T(8,128)S(1)}, f32[4,4,64,64]{3,2,1,0:T(8,128)}, u32[]{:S(2)}) %copy-start.6) | copy-done | bytes 262168
  49.7 0.0 copy-start.9
  49.7 0.9 %copy-done.9 = f32[4,2,64,64]{3,2,1,0:T(8,128)S(1)} copy-done((f32[4,2,64,64]{3,2,1,0:T(8,128)S(1)}, f32[4,2,64,64]{3,2,1,0:T(8,128)}, u32[]{:S(2)}) %copy-start.9) | copy-done | bytes 131096
  50.6 0.0 copy-start.11
  50.6 0.8 %copy-done.11 = f32[64,64]{1,0:T(8,128)S(1)} copy-done((f32[64,64]{1,0:T(8,128)S(1)}, f32[64,64]{1,0:T(8,128)}, u32[]{:S(2)}) %copy-start.11) | copy-done | bytes 16408
  51.4 0.0 copy-start.15
  51.4 0.7 %copy-done.15 = s32[1,4,4]{2,1,0:T(4,128)S(1)} copy-done((s32[1,4,4]{2,1,0:T(4,128)S(1)}, s32[1,4,4]{2,1,0:T(4,128)}, u32[]{:S(2)}) %copy-start.15) | copy-done | bytes 88
  52.1 0.0 copy-start.16
  52.1 0.7 %copy-done.16 = s32[8]{0:T(128)S(1)} copy-done((s32[8]{0:T(128)S(1)}, s32[8]{0:T(128)}, u32[]{:S(2)}) %copy-start.16) | copy-done | bytes 56
  52.7 6.2 %down.1 = f32[16,2048]{1,0:T(8,128)} custom-call(s32[1]{0:T(128)} %bitcast.me_ref, s32[8,3]{1,0:T(8,128)S(1)} %copy.18.ids_ref.near_ids_ref, s32[8,8]{1,0:T(8,128)S(1)} %copy-done.14, s32[8]{0:T(128)S(1)} %copy-done.16, s32[4,4]{1,0:T(4,128)S(1)} %bitcast.18, f32[8,96,128]{2,1,0:T(8,128)S(1)} %all_to_all.16.near_in, ...), custom_call_target="tpu_custom_call" | custom-call | tf_op jit(solution)/shard_map/down/pallas_call | solution.py:356
Async XLA Ops:
  0.0 46.8 %copy-start.14 = (s32[8,8]{1,0:T(8,128)S(1)}, s32[8,8]{1,0:T(8,128)}, u32[]{:S(2)}) copy-start(s32[8,8]{1,0:T(8,128)} %far_ids_ref.1) | copy-start | bytes 772
  0.0 1.1 %copy-start = (f32[8,256,64]{1,2,0:T(8,128)S(1)}, f32[8,256,64]{1,2,0:T(8,128)}, u32[]{:S(2)}) copy-start(f32[8,256,64]{1,2,0:T(8,128)} %param.15) | copy-start | bytes 1572868
  1.1 0.9 %copy-start.3 = (f32[8,64,64]{2,1,0:T(8,128)S(1)}, f32[8,64,64]{2,1,0:T(8,128)}, u32[]{:S(2)}) copy-start(f32[8,64,64]{2,1,0:T(8,128)} %lift_ref.3) | copy-start | bytes 393220
  2.0 0.9 %copy-start.10 = (f32[16,2048]{1,0:T(8,128)S(1)}, f32[16,2048]{1,0:T(8,128)}, u32[]{:S(2)}) copy-start(f32[16,2048]{1,0:T(8,128)} %points_ref.1) | copy-start | bytes 393220
  2.9 0.7 %copy-start.12 = (s32[2048]{0:T(1024)S(1)}, s32[2048]{0:T(1024)}, u32[]{:S(2)}) copy-start(s32[2048]{0:T(1024)} %param.14) | copy-start | bytes 24580
  3.6 43.2 %copy-start.1 = (f32[8,256,64]{1,2,0:T(8,128)S(1)}, f32[8,256,64]{1,2,0:T(8,128)}, u32[]{:S(2)}) copy-start(f32[8,256,64]{1,2,0:T(8,128)} %param.15) | copy-start | bytes 1572868
  3.6 43.2 %copy-start.2 = (f32[8,8,64,64]{3,2,1,0:T(8,128)S(1)}, f32[8,8,64,64]{3,2,1,0:T(8,128)}, u32[]{:S(2)}) copy-start(f32[8,8,64,64]{3,2,1,0:T(8,128)} %far_ref.1) | copy-start | bytes 3145732
  4.9 26.2 %copy-start.8 = (f32[8,96,128]{2,1,0:T(8,128)}, f32[8,96,128]{2,1,0:T(8,128)S(1)}, u32[]{:S(2)}) copy-start(f32[8,96,128]{2,1,0:T(8,128)S(1)} %get-tuple-element.10) | copy-start | bytes 1179652
  31.1 15.7 %all-to-all-start.1 = ((f32[8,96,128]{2,1,0:T(8,128)}), f32[8,96,128]{2,1,0:T(8,128)S(1)}, u32[]{:S(2)}, u32[]{:S(2)}) async-start(f32[8,96,128]{2,1,0:T(8,128)} %copy-done.8), calls=%async_computation.1 | async-start | bytes 786432 | tf_op jit(solution)/shard_map/all_to_all | solution.py:318
  38.5 0.7 %copy-start.13 = (s32[2048]{0:T(1024)S(1)}, s32[2048]{0:T(1024)}, u32[]{:S(2)}) copy-start(s32[2048]{0:T(1024)} %param.14) | copy-start | bytes 24580
  39.5 0.9 %copy-start.7 = (f32[2,8,8,256]{3,2,0,1:T(8,128)S(1)}, f32[2,8,8,256]{3,2,0,1:T(8,128)}, u32[]{:S(2)}) copy-start(f32[2,8,8,256]{3,2,0,1:T(8,128)} %copy.21) | copy-start | bytes 393220
  46.8 1.0 %copy-start.4 = (f32[8,64,64]{2,1,0:T(8,128)S(1)}, f32[8,64,64]{2,1,0:T(8,128)}, u32[]{:S(2)}) copy-start(f32[8,64,64]{2,1,0:T(8,128)} %lift_ref.3) | copy-start | bytes 393220
  47.7 0.9 %copy-start.5 = (f32[32,8,128]{2,1,0:T(8,128)S(1)}, f32[32,8,128]{2,1,0:T(8,128)}, u32[]{:S(2)}) copy-start(f32[32,8,128]{2,1,0:T(8,128)} %all_to_all.15.nodes_in) | copy-start | bytes 393220
  48.6 1.0 %copy-start.6 = (f32[4,4,64,64]{3,2,1,0:T(8,128)S(1)}, f32[4,4,64,64]{3,2,1,0:T(8,128)}, u32[]{:S(2)}) copy-start(f32[4,4,64,64]{3,2,1,0:T(8,128)} %couple_ref.1) | copy-start | bytes 786436
  49.7 0.9 %copy-start.9 = (f32[4,2,64,64]{3,2,1,0:T(8,128)S(1)}, f32[4,2,64,64]{3,2,1,0:T(8,128)}, u32[]{:S(2)}) copy-start(f32[4,2,64,64]{3,2,1,0:T(8,128)} %transfer_ref.1) | copy-start | bytes 393220
  50.6 0.8 %copy-start.11 = (f32[64,64]{1,0:T(8,128)S(1)}, f32[64,64]{1,0:T(8,128)}, u32[]{:S(2)}) copy-start(f32[64,64]{1,0:T(8,128)} %top_ref.1) | copy-start | bytes 49156
  51.4 0.7 %copy-start.15 = (s32[1,4,4]{2,1,0:T(4,128)S(1)}, s32[1,4,4]{2,1,0:T(4,128)}, u32[]{:S(2)}) copy-start(s32[1,4,4]{2,1,0:T(4,128)} %param.24) | copy-start | bytes 196
  52.1 0.7 %copy-start.16 = (s32[8]{0:T(128)S(1)}, s32[8]{0:T(128)}, u32[]{:S(2)}) copy-start(s32[8]{0:T(128)} %far_count_ref.1) | copy-start | bytes 100

commit v2 on v0

v2 whole, which is shorter than its diff:
```python
import functools

import jax
import jax.numpy as jnp
from jax import lax
from jax.experimental import pallas as pl
from jax.experimental.pallas import tpu as pltpu
from jax.sharding import PartitionSpec as P

REACH = 4
DEPTH = 4
OFFSETS = (-3, -2, 2, 3)
GROUP = 2 * REACH
LANES = 128
TILE = 8
VMEM_LIMIT = 24 * 1024 * 1024

NN = (((1,), (0,)), ((), ()))
NT = (((1,), (1,)), ((), ()))

VMEM = pl.BlockSpec(memory_space=pltpu.VMEM)
SMEM = pl.BlockSpec(memory_space=pltpu.SMEM)
HBM = pl.BlockSpec(memory_space=pltpu.HBM)
PARAMS = pltpu.CompilerParams(vmem_limit_bytes=VMEM_LIMIT)
F32 = jnp.float32
BF16 = jnp.bfloat16


def halves(x):
    high = x.astype(BF16)
    low = (x - high.astype(F32)).astype(BF16)
    return high, low


def dot_halves(a, b_high, b_low, dims):
    a_high, a_low = halves(a)
    rows = a.shape[0]
    both = lax.dot_general(
        jnp.concatenate([a_high, a_low], axis=0), b_high, dims, preferred_element_type=F32
    )
    cross = lax.dot_general(a_high, b_low, dims, preferred_element_type=F32)
    return both[:rows] + (both[rows:] + cross)


def dot3(a, b, dims):
    return dot_halves(a, *halves(b), dims)


def fold(x):
    return jnp.concatenate([x[:TILE], x[TILE:]], axis=1)


def beside(p, q):
    rank = p.shape[1] // 2
    left = lax.broadcasted_iota(jnp.int32, p.shape, 1) < rank
    return jnp.concatenate(
        [
            jnp.where(left, p, pltpu.roll(q, rank, 1)),
            jnp.where(left, pltpu.roll(p, rank, 1), q),
        ],
        axis=0,
    )


def row_of(tiles):
    return jnp.concatenate([beside(*tiles[k : k + 2]) for k in range(0, len(tiles), 2)], axis=1)


def lane_gather(x, high, low):
    rows, columns = x.shape
    high = jnp.broadcast_to(high, (rows, LANES))
    low = jnp.broadcast_to(low, (rows, LANES))
    result = jnp.zeros((rows, LANES), x.dtype)
    for source in range(columns // LANES):
        tile = x[:, source * LANES : (source + 1) * LANES]
        moved = jnp.take_along_axis(tile, low, axis=1, mode="promise_in_bounds")
        result = jnp.where(high == source, moved, result)
    return result


def fetch(pairs, sems):
    copies = [
        pltpu.make_async_copy(source, target, sems.at[index])
        for index, (source, target) in enumerate(pairs)
    ]
    for copy in copies:
        copy.start()
    return copies


def up_kernel(
    me_ref, points_hbm, order_hbm, bases_hbm, lift_hbm, out, x_out, points_v, order_v, bases_v, lift_v, sems
):
    copies = fetch(
        [(order_hbm, order_v), (points_hbm, points_v), (bases_hbm, bases_v), (lift_hbm, lift_v)], sems
    )
    me = me_ref[0]
    leaf_dev, rank, leaf_size = bases_v.shape
    vectors, points_dev = points_v.shape
    copies[0].wait()
    copies[1].wait()
    points = points_v[...]
    per_leaf = leaf_size // LANES
    for t in range(points_dev // LANES):
        spot = order_v[t : t + 1, :] - me * points_dev
        column = t % per_leaf * LANES
        x_out[t // per_leaf, :, column : column + LANES] = lane_gather(
            points, lax.shift_right_logical(spot, 7), spot & (LANES - 1)
        )
    copies[2].wait()
    coefs = [dot3(x_out[leaf], bases_v[leaf], NT) for leaf in range(leaf_dev)]
    tiles = [fold(coef) for coef in coefs]
    copies[3].wait()
    weights = lift_v[...].reshape(leaf_dev * rank, rank)
    tiles.append(fold(dot3(jnp.concatenate(coefs, axis=1), weights, NN)))
    for peer in range(GROUP):
        for index, tile in enumerate(tiles):
            out[peer, index * TILE : (index + 1) * TILE, :] = tile
    place = lax.rem(me, GROUP)
    start = len(tiles) * TILE
    for part in range(per_leaf):
        first = x_out[0, :, part * LANES : (part + 1) * LANES]
        last = x_out[leaf_dev - 1, :, part * LANES : (part + 1) * LANES]
        rows = slice(start + part * vectors, start + (part + 1) * vectors)
        for peer in range(GROUP):
            above = lax.rem(place + 1, GROUP) == peer
            out[peer, rows, :] = jnp.where(above, last, first)


def side_kernel(
    me_ref,
    x_ref,
    order_hbm,
    ids_hbm,
    links_hbm,
    blocks_hbm,
    bases_hbm,
    lift_hbm,
    far_hbm,
    transfer_hbm,
    couple_hbm,
    top_hbm,
    near_out,
    inverse_out,
    edge_high,
    edge_low,
    leaf_high,
    leaf_low,
    bases_high,
    bases_low,
    up_high,
    up_low,
    path_high,
    path_low,
    order_v,
    ids_s,
    links_s,
    blocks_v,
    bases_v,
    lift_v,
    far_v,
    transfer_v,
    couple_v,
    top_v,
    sems,
    block_sems,
):
    me = me_ref[0]
    leaf_dev, slots, leaf_size, _ = blocks_v.shape
    _, rank, _ = bases_v.shape
    small = fetch(
        [
            (ids_hbm, ids_s),
            (links_hbm, links_s),
            (order_hbm, order_v),
            (transfer_hbm, transfer_v),
            (couple_hbm, couple_v),
            (top_hbm, top_v),
            (lift_hbm, lift_v),
            (far_hbm, far_v),
            (bases_hbm, bases_v),
        ],
        sems,
    )
    blocks = fetch([(blocks_hbm.at[leaf], blocks_v.at[leaf]) for leaf in range(leaf_dev)], block_sems)
    for copy in small:
        copy.wait()

    points_dev = order_v.shape[1]
    tiles = points_dev // LANES
    spot = order_v[...] - me * points_dev
    times = lax.broadcasted_iota(jnp.int32, (1, points_dev), 1)
    shape = (tiles, points_dev)
    match = lax.broadcasted_iota(jnp.int32, shape, 0) == lax.shift_right_logical(spot, 7)
    digits = [
        jnp.where(match, jnp.broadcast_to(digit.astype(F32), shape), 0.0)
        for digit in (lax.shift_right_logical(times, 4), times & 15)
    ]
    shape = (LANES, points_dev)
    match = lax.broadcasted_iota(jnp.int32, shape, 0) == (spot & (LANES - 1))
    both = lax.dot_general(
        jnp.concatenate(digits, axis=0).astype(BF16),
        jnp.where(match, 1.0, 0.0).astype(BF16),
        NT,
        preferred_element_type=F32,
    )
    inverse_out[...] = (both[:tiles] * 16.0 + both[tiles:]).astype(jnp.int32)

    composed = transfer_v[0].reshape(2 * rank, rank)
    row = 0
    for level in range(1, DEPTH):
        rows = composed.shape[0]
        up_high[row : row + rows], up_low[row : row + rows] = halves(composed)
        row += rows
        if level < DEPTH - 1:
            composed = jnp.concatenate(
                [dot3(composed, transfer_v[level, side], NN) for side in range(2)], axis=0
            )

    path = None
    for level in range(DEPTH):
        weights = []
        for column in range(len(OFFSETS)):
            link = links_s[level, column].astype(F32)
            weights.append(link * couple_v[level, column])
        weights = jnp.concatenate(weights, axis=1)
        step = transfer_v[level, lax.shift_right_logical(me, level) & 1]
        if path is not None:
            weights = dot3(path, weights, NN)
            step = dot3(path, step, NN)
        path = step
        column = level * len(OFFSETS) * rank
        span = slice(column, column + weights.shape[1])
        path_high[:, span], path_low[:, span] = halves(weights)
    top = dot3(path, top_v[...], NN)
    last = jnp.concatenate(
        [dot3(top, transfer_v[DEPTH - 1, side], NT) for side in range(2)], axis=1
    )
    column = DEPTH * len(OFFSETS) * rank
    span = slice(column, column + 2 * rank)
    path_high[:, span], path_low[:, span] = halves(last)

    for leaf in range(leaf_dev):
        row = [far_v[leaf, slot] for slot in range(far_v.shape[1])] + [lift_v[leaf]]
        leaf_high[leaf], leaf_low[leaf] = halves(jnp.concatenate(row, axis=1))
        bases_high[leaf], bases_low[leaf] = halves(bases_v[leaf])

    for copy in blocks:
        copy.wait()

    def near(leaf, carry):
        total = jnp.zeros(near_out.shape[1:], F32)
        for slot in range(slots):
            local = ids_s[slot, leaf] - me * leaf_dev
            here = (local >= 0) & (local < leaf_dev)
            x_leaf = jnp.where(here, x_ref[jnp.clip(local, 0, leaf_dev - 1)], 0.0)
            total = total + dot3(x_leaf, blocks_v[leaf, slot], NT)
        near_out[leaf] = total
        return carry

    lax.fori_loop(0, leaf_dev, near, 0)

    for index, leaf, outside in ((0, 0, -1), (1, leaf_dev - 1, leaf_dev)):
        total = jnp.zeros((leaf_size, leaf_size), F32)
        for slot in range(1, slots):
            remote = ids_s[slot, leaf] - me * leaf_dev == outside
            total = total + jnp.where(remote, blocks_v[leaf, slot], 0.0)
        edge_high[index], edge_low[index] = halves(total)


def middle_kernel(me_ref, group_ref, up_high, up_low, nodes_out, half_out):
    place = lax.rem(me_ref[0], GROUP)
    roots = [group_ref[peer, 8 * TILE : 9 * TILE, :] for peer in range(GROUP)]
    start, index = 0, 0
    for level in range(1, DEPTH):
        width = 1 << level
        count = GROUP // width
        left = jnp.concatenate(
            [row_of(roots[n * width : (n + 1) * width]) for n in range(count)], axis=0
        )
        size = left.shape[1]
        nodes = dot_halves(left, up_high[start : start + size], up_low[start : start + size], NN)
        start += size
        for n in range(count):
            nodes_out[index] = fold(nodes[n * 2 * TILE : (n + 1) * 2 * TILE])
            index += 1
    nodes_out[index] = jnp.zeros((TILE, LANES), F32)
    low = place < REACH
    for part in range(REACH):
        chosen = group_ref[jnp.where(low, REACH, 0) + part, : 9 * TILE]
        half_out[part * 9 * TILE : (part + 1) * 9 * TILE] = chosen
    half_out[REACH * 9 * TILE :] = group_ref[jnp.where(low, GROUP - 1, 0), 9 * TILE :]


def down_kernel(
    me_ref,
    group_ref,
    half_ref,
    nodes_ref,
    near_ref,
    inverse_ref,
    edge_high,
    edge_low,
    leaf_high,
    leaf_low,
    bases_high,
    bases_low,
    path_high,
    path_low,
    far_ids_hbm,
    far_count_hbm,
    out_ref,
    far_ids_s,
    far_count_s,
    y_tree,
    sems,
):
    copies = fetch([(far_ids_hbm, far_ids_s), (far_count_hbm, far_count_s)], sems)
    me = me_ref[0]
    leaf_dev, vectors, leaf_size = near_ref.shape
    points_dev = out_ref.shape[1]
    groups = nodes_ref.shape[0]
    slots = far_ids_s.shape[1]
    group = lax.shift_right_logical(me, 3)
    place = me & (GROUP - 1)
    low = place < REACH
    per_leaf = leaf_size // LANES
    start = (leaf_dev + 1) * TILE

    def tile_of(subtree, index):
        other = subtree & (GROUP - 1)
        inside = lax.shift_right_arithmetic(subtree, 3) == group
        row = pl.multiple_of(index * TILE, TILE)
        near_row = jnp.clip(other - jnp.where(low, REACH, 0), 0, REACH - 1) * start
        here = group_ref[other, pl.ds(row, TILE), :]
        there = half_ref[pl.ds(pl.multiple_of(near_row + row, TILE), TILE), :]
        return jnp.where(inside, here, there)

    partners = []
    for level in range(DEPTH):
        node = lax.shift_right_logical(me, level)
        size = (groups * GROUP) >> level
        for offset in OFFSETS:
            other = node + offset
            used = (other >= 0) & (other < size)
            other = jnp.clip(other, 0, size - 1)
            if level == 0:
                tile = tile_of(other, leaf_dev)
            else:
                shift = DEPTH - 1 - level
                first = GROUP - (2 << shift)
                tile = nodes_ref[
                    lax.shift_right_logical(other, shift), first + (other & ((1 << shift) - 1))
                ]
            partners.append(jnp.where(used, tile, 0.0))
    top = lax.shift_right_logical(me, DEPTH)
    for side in range(2):
        blended = jnp.zeros((TILE, LANES), F32)
        for other in range(groups // 2):
            distance = jnp.abs(top - other)
            weight = jnp.where(distance >= 2, 1.0 / jnp.maximum(distance, 1).astype(F32), 0.0)
            blended = blended + weight * nodes_ref[2 * other + side, GROUP - 2]
        partners.append(blended)
    down = dot_halves(row_of(partners), path_high[...], path_low[...], NT)

    edges = []
    for index, offset in ((0, -1), (1, 1)):
        other = me + offset
        inside = lax.shift_right_arithmetic(other, 3) == group
        here = group_ref[other & (GROUP - 1), start:, :]
        chosen = jnp.where(inside, here, half_ref[REACH * start :, :])
        edges.append(
            jnp.concatenate(
                [chosen[part * vectors : (part + 1) * vectors] for part in range(per_leaf)], axis=1
            )
        )
    edge_parts = [
        dot_halves(edges[index], edge_high[index], edge_low[index], NT) for index in range(2)
    ]

    for copy in copies:
        copy.wait()
    for leaf in range(leaf_dev):
        picked = []
        for slot in range(slots):
            used = slot < far_count_s[leaf]
            spot = far_ids_s[leaf, slot]
            tile = tile_of(lax.shift_right_logical(spot, 3), spot & (leaf_dev - 1))
            picked.append(jnp.where(used, tile, 0.0))
        left = jnp.concatenate([row_of(picked), down], axis=1)
        leaf_out = dot_halves(left, leaf_high[leaf], leaf_low[leaf], NT)
        y_leaf = near_ref[leaf] + dot_halves(leaf_out, bases_high[leaf], bases_low[leaf], NN)
        if leaf == 0:
            y_leaf = y_leaf + edge_parts[0]
        if leaf == leaf_dev - 1:
            y_leaf = y_leaf + edge_parts[1]
        y_tree[:, leaf * leaf_size : (leaf + 1) * leaf_size] = y_leaf

    y = y_tree[...]
    for tile in range(points_dev // LANES):
        spot = inverse_ref[tile : tile + 1, :]
        out_ref[:, tile * LANES : (tile + 1) * LANES] = lane_gather(
            y, lax.shift_right_logical(spot, 7), spot & (LANES - 1)
        )


def local(
    devices,
    points,
    order,
    bases,
    lift,
    near_ids,
    near_blocks,
    far_ids,
    far_count,
    far_blocks,
    transfer,
    couple,
    links,
    top_couple,
):
    me = lax.axis_index("leaf").astype(jnp.int32).reshape(1)
    vectors, points_dev = points.shape
    leaf_dev, leaf_size, rank = bases.shape
    slots = near_ids.shape[1]
    far_slots = far_ids.shape[1]
    bases_t = jnp.swapaxes(bases, 1, 2)
    tiles = points_dev // LANES
    edge_rows = vectors * (leaf_size // LANES)
    rows = (leaf_dev + 1) * TILE
    groups = devices // GROUP
    order_tiles = order.reshape(tiles, LANES)
    shape = jax.ShapeDtypeStruct

    group_out, tree_x = pl.pallas_call(
        up_kernel,
        out_shape=[
            shape((GROUP, rows + edge_rows, LANES), F32),
            shape((leaf_dev, vectors, leaf_size), F32),
        ],
        in_specs=[SMEM] + [HBM] * 4,
        out_specs=[VMEM] * 2,
        scratch_shapes=[
            pltpu.VMEM(points.shape, F32),
            pltpu.VMEM((tiles, LANES), jnp.int32),
            pltpu.VMEM(bases_t.shape, F32),
            pltpu.VMEM(lift.shape, F32),
            pltpu.SemaphoreType.DMA((4,)),
        ],
        compiler_params=PARAMS,
        name="up",
    )(me, points, order_tiles, bases_t, lift)

    aligned = [[g * GROUP + i for i in range(GROUP)] for g in range(groups)]
    group_in = lax.all_to_all(group_out, "leaf", 0, 0, axis_index_groups=aligned, tiled=True)

    ids_t = near_ids.T
    links_own = links.reshape(links.shape[1:])
    composed_rows = (2 + 4 + 8) * rank
    path_columns = (DEPTH * len(OFFSETS) + 2) * rank
    leaf_columns = (far_slots + 1) * rank
    both = lambda *size: [shape(size, BF16)] * 2
    operands = (
        order.reshape(1, points_dev),
        ids_t,
        links_own,
        near_blocks,
        bases_t,
        lift,
        far_blocks,
        transfer,
        couple,
        top_couple,
    )
    (
        near_part,
        inverse,
        edge_high,
        edge_low,
        leaf_high,
        leaf_low,
        bases_high,
        bases_low,
        up_high,
        up_low,
        path_high,
        path_low,
    ) = pl.pallas_call(
        side_kernel,
        out_shape=[shape(tree_x.shape, F32), shape((tiles, LANES), jnp.int32)]
        + both(2, leaf_size, leaf_size)
        + both(leaf_dev, rank, leaf_columns)
        + both(leaf_dev, rank, leaf_size)
        + both(composed_rows, rank)
        + both(rank, path_columns),
        in_specs=[SMEM, VMEM] + [HBM] * len(operands),
        out_specs=[VMEM] * 12,
        scratch_shapes=[
            (pltpu.SMEM if x is ids_t or x is links_own else pltpu.VMEM)(x.shape, x.dtype)
            for x in operands
        ]
        + [pltpu.SemaphoreType.DMA((len(operands) - 1,)), pltpu.SemaphoreType.DMA((leaf_dev,))],
        compiler_params=PARAMS,
        cost_estimate=pl.CostEstimate(
            flops=6 * vectors * near_blocks.size,
            bytes_accessed=4 * near_blocks.size,
            transcendentals=0,
        ),
        name="side",
    )(me, tree_x, *operands)

    nodes_out, half_out = pl.pallas_call(
        middle_kernel,
        out_shape=[shape((GROUP, TILE, LANES), F32), shape((REACH * rows + edge_rows, LANES), F32)],
        in_specs=[SMEM] + [VMEM] * 3,
        out_specs=[VMEM] * 2,
        compiler_params=PARAMS,
        name="middle",
    )(me, group_in, up_high, up_low)

    pairs = []
    for device in range(devices):
        target = device + GROUP if device % GROUP < REACH else device - GROUP
        if 0 <= target < devices:
            pairs.append((device, target))
    half_in = lax.ppermute(half_out, "leaf", pairs)
    across = [[g * GROUP + i for g in range(groups)] for i in range(GROUP)]
    nodes_in = lax.all_gather(nodes_out, "leaf", axis=0, axis_index_groups=across)

    return pl.pallas_call(
        down_kernel,
        out_shape=shape((vectors, points_dev), F32),
        in_specs=[SMEM] + [VMEM] * 13 + [HBM] * 2,
        out_specs=VMEM,
        scratch_shapes=[
            pltpu.SMEM(far_ids.shape, jnp.int32),
            pltpu.SMEM(far_count.shape, jnp.int32),
            pltpu.VMEM((vectors, points_dev), F32),
            pltpu.SemaphoreType.DMA((2,)),
        ],
        compiler_params=PARAMS,
        name="down",
    )(
        me,
        group_in,
        half_in,
        nodes_in,
        near_part,
        inverse,
        edge_high,
        edge_low,
        leaf_high,
        leaf_low,
        bases_high,
        bases_low,
        path_high,
        path_low,
        far_ids,
        far_count,
    )


def solution(mesh):
    in_specs = (
        P(None, "leaf"),
        P("leaf"),
        P("leaf", None, None),
        P("leaf", None, None),
        P("leaf", None),
        P("leaf", None, None, None),
        P("leaf", None),
        P("leaf"),
        P("leaf", None, None, None),
        P(),
        P(),
        P("leaf", None, None),
        P(),
    )
    return jax.shard_map(
        functools.partial(local, mesh.shape["leaf"]),
        mesh=mesh,
        in_specs=in_specs,
        out_specs=P(None, "leaf"),
        check_vma=False,
    )
```

time: 184 us -> 52.3 us (0.28); the launches traced: 181 us -> 51.5 us
  blocking collectives: 75.7 us -> 13.6 us
  matrix products: 38.8 us -> 0 us
  starting transfers between devices: 23.8 us -> 8.66 us
  Pallas kernels: 0 us -> 11.4 us
  local copies, waits for them, and re-layouts: 28.5 us -> 17.9 us
  waiting for transfers between devices: 8.32 us -> 0.01 us
  other arithmetic: 5.64 us -> 0 us
    all_gather x2 -> x1, blocking collectives: 75.7 us -> 13.6 us  [local(): lax.all_gather(nodes_out, 'leaf', axis=0, axis_index_groups=across)]
    dot_general x40 -> x0, matrix products: 38.8 us -> none  [the longest x16 17.1 us: full_tree(): jnp.einsum('qr,nrs->nqs', couple[level, column], partner, precision=HIGHE...]
    ppermute x10 -> x1, starting transfers between devices: 23.8 us -> 3.49 us  [local(): half_in = lax.ppermute(half_out, 'leaf', pairs)]
    unnamed x30 -> x40, local copies, waits for them, and re-layouts: 5.65 us -> 17.9 us
    pallas_call x0 -> x4, Pallas kernels: none -> 11.4 us  [the longest x1 5.02 us: local(): pl.pallas_call(side_kernel, out_shape=[shape(tree_x.shape, F32), shape((t...]
    ppermute x10 -> x1, waiting for transfers between devices: 8.32 us -> 0.01 us  [local(): half_in = lax.ppermute(half_out, 'leaf', pairs)]
    gather x4 -> x0, local copies, waits for them, and re-layouts: 8.18 us -> none  [the longest x2 6.98 us: local(): tree_x = jnp.take(points, local_order, axis=1)]
    scatter x2 -> x0, local copies, waits for them, and re-layouts: 7.17 us -> none  [local(): jnp.zeros((vectors, points_dev), jnp.float32).at[:, local_order].set(tree_y)]
  transfers between devices with their start and end apart: 10 -> 2, of which waited for: 3 -> 0; matrix products, arithmetic and copies ran while one was open for 27% -> 0% of each run, Pallas kernels for 0% -> 10%
where the time goes in v2:
time: 52.3 us; the launch traced here: 51.5 us
  local copies, waits for them, and re-layouts  17.9 us (34%)
  blocking collectives  13.6 us (26%)
  Pallas kernels  11.4 us (22%)
  starting transfers between devices  8.66 us (17%)
    unnamed x40, local copies, waits for them, and re-layouts  17.9 us
    all_gather x1, blocking collectives, local(): lax.all_gather(nodes_out, 'leaf', axis=0, axis_index_groups=across)  13.6 us
    all_to_all x1, starting transfers between devices, local(): lax.all_to_all(group_out, 'leaf', 0, 0, axis_index_groups=aligned, tiled=...  5.17 us
    pallas_call x1, Pallas kernels, local(): pl.pallas_call(side_kernel, out_shape=[shape(tree_x.shape, F32), shape((t...  5.02 us
    pallas_call x1, Pallas kernels, local(): pl.pallas_call(down_kernel, out_shape=shape((vectors, points_dev), F32),...  3.73 us
    ppermute x1, starting transfers between devices, local(): half_in = lax.ppermute(half_out, 'leaf', pairs)  3.49 us
    pallas_call x1, Pallas kernels, local(): pl.pallas_call(up_kernel, out_shape=[shape((GROUP, rows + edge_rows, LANE...  2.29 us
  transfers between devices with their start and end apart: 2, of which 0 were waited for; matrix products, arithmetic and copies ran while one was open for 0% of the time, Pallas kernels for 10%

profile of v2, /device:TPU:0, one launch (start us, length us, event | category | flops | bytes accessed | tf_op | source)
XLA Modules:
  0.0 51.5 jit_solution(10091204551712210383)
XLA Ops:
  0.0 0.0 copy-start.1
  0.0 1.0 %copy-done.1 = f32[8,256,64]{1,2,0:T(8,128)S(1)} copy-done((f32[8,256,64]{1,2,0:T(8,128)S(1)}, f32[8,256,64]{1,2,0:T(8,128)}, u32[]{:S(2)}) %copy-start.1) | copy-done | bytes 524312
  1.0 0.0 copy-start.4
  1.0 0.9 %copy-done.4 = f32[8,64,64]{2,1,0:T(8,128)S(1)} copy-done((f32[8,64,64]{2,1,0:T(8,128)S(1)}, f32[8,64,64]{2,1,0:T(8,128)}, u32[]{:S(2)}) %copy-start.4) | copy-done | bytes 131096
  2.0 0.0 copy-start.10
  2.0 0.9 %copy-done.10 = f32[16,2048]{1,0:T(8,128)S(1)} copy-done((f32[16,2048]{1,0:T(8,128)S(1)}, f32[16,2048]{1,0:T(8,128)}, u32[]{:S(2)}) %copy-start.10) | copy-done | bytes 131096
  2.9 0.0 copy-start.14
  2.9 0.7 %copy-done.14 = s32[2048]{0:T(1024)S(1)} copy-done((s32[2048]{0:T(1024)S(1)}, s32[2048]{0:T(1024)}, u32[]{:S(2)}) %copy-start.14) | copy-done | bytes 8216
  3.6 0.0 copy-start.16
  3.6 0.0 copy-start.19
  3.6 2.3 %up.1 = (f32[8,104,128]{2,1,0:T(8,128)}, f32[8,16,256]{2,1,0:T(8,128)S(1)}) custom-call(s32[1]{0:T(128)} %bitcast.me_ref, f32[16,2048]{1,0:T(8,128)S(1)} %copy-done.10, s32[16,128]{1,0:T(8,128)S(1)} %bitcast.10, f32[8,64,256]{2,1,0:T(8,128)S(1)} %bitcast.7, f32[8,64,64]{2,1,0:T(8,128)S(1)} %copy-done.4), custom_call_target="tpu_custom_call" | custom-call | tf_op jit(solution)/shard_map/up/pallas_call | solution.py:436
  5.9 0.0 copy-start.8
  5.9 0.6 %copy-done.8 = f32[8,16,256]{2,1,0:T(8,128)} copy-done((f32[8,16,256]{2,1,0:T(8,128)}, f32[8,16,256]{2,1,0:T(8,128)S(1)}, u32[]{:S(2)}) %copy-start.8) | copy-done | bytes 131096
  6.6 5.2 %all-to-all-start = ((f32[8,104,128]{2,1,0:T(8,128)}), f32[8,104,128]{2,1,0:T(8,128)S(1)}, u32[]{:S(2)}, u32[]{:S(2)}) async-start(f32[8,104,128]{2,1,0:T(8,128)} %get-tuple-element.21), calls=%async_computation | async-start | bytes 851968 | tf_op jit(solution)/shard_map/all_to_all | solution.py:456
  11.7 0.0 copy-start
  11.7 2.8 %copy-done = f32[8,3,256,256]{3,2,1,0:T(8,128)S(1)} copy-done((f32[8,3,256,256]{3,2,1,0:T(8,128)S(1)}, f32[8,3,256,256]{3,2,1,0:T(8,128)}, u32[]{:S(2)}) %copy-start) | copy-done | bytes 6291480
  14.5 0.0 copy-start.2
  14.5 1.0 %copy-done.2 = f32[8,256,64]{1,2,0:T(8,128)S(1)} copy-done((f32[8,256,64]{1,2,0:T(8,128)S(1)}, f32[8,256,64]{1,2,0:T(8,128)}, u32[]{:S(2)}) %copy-start.2) | copy-done | bytes 524312
  15.6 0.0 copy-start.3
  15.6 1.6 %copy-done.3 = f32[8,8,64,64]{3,2,1,0:T(8,128)S(1)} copy-done((f32[8,8,64,64]{3,2,1,0:T(8,128)S(1)}, f32[8,8,64,64]{3,2,1,0:T(8,128)}, u32[]{:S(2)}) %copy-start.3) | copy-done | bytes 1048600
  17.1 0.0 copy-start.5
  17.1 0.9 %copy-done.5 = f32[8,64,64]{2,1,0:T(8,128)S(1)} copy-done((f32[8,64,64]{2,1,0:T(8,128)S(1)}, f32[8,64,64]{2,1,0:T(8,128)}, u32[]{:S(2)}) %copy-start.5) | copy-done | bytes 131096
  18.1 0.0 copy-start.6
  18.1 1.0 %copy-done.6 = f32[4,4,64,64]{3,2,1,0:T(8,128)S(1)} copy-done((f32[4,4,64,64]{3,2,1,0:T(8,128)S(1)}, f32[4,4,64,64]{3,2,1,0:T(8,128)}, u32[]{:S(2)}) %copy-start.6) | copy-done | bytes 262168
  19.1 0.0 copy-start.7
  19.1 0.9 %copy-done.7 = f32[4,2,64,64]{3,2,1,0:T(8,128)S(1)} copy-done((f32[4,2,64,64]{3,2,1,0:T(8,128)S(1)}, f32[4,2,64,64]{3,2,1,0:T(8,128)}, u32[]{:S(2)}) %copy-start.7) | copy-done | bytes 131096
  20.1 0.0 copy-start.9
  20.1 0.9 %copy-done.9 = f32[8,16,256]{2,1,0:T(8,128)S(1)} copy-done((f32[8,16,256]{2,1,0:T(8,128)S(1)}, f32[8,16,256]{2,1,0:T(8,128)}, u32[]{:S(2)}) %copy-start.9) | copy-done | bytes 131096
  21.0 0.0 copy-start.13
  21.0 0.8 %copy-done.13 = f32[64,64]{1,0:T(8,128)S(1)} copy-done((f32[64,64]{1,0:T(8,128)S(1)}, f32[64,64]{1,0:T(8,128)}, u32[]{:S(2)}) %copy-start.13) | copy-done | bytes 16408
  21.8 0.0 copy-start.15
  21.8 0.7 %copy-done.15 = s32[2048]{0:T(1024)S(1)} copy-done((s32[2048]{0:T(1024)S(1)}, s32[2048]{0:T(1024)}, u32[]{:S(2)}) %copy-start.15) | copy-done | bytes 8216
  22.4 0.0 copy-start.17
  22.5 0.7 %copy-done.17 = s32[8,3]{0,1:T(4,128)S(1)} copy-done((s32[8,3]{0,1:T(4,128)S(1)}, s32[8,3]{0,1:T(4,128)}, u32[]{:S(2)}) %copy-start.17) | copy-done | bytes 120
  23.1 0.0 copy-start.18
  23.1 0.7 %copy-done.18 = s32[1,4,4]{2,1,0:T(4,128)S(1)} copy-done((s32[1,4,4]{2,1,0:T(4,128)S(1)}, s32[1,4,4]{2,1,0:T(4,128)}, u32[]{:S(2)}) %copy-start.18) | copy-done | bytes 88
  23.8 5.0 %side.1 = (f32[8,16,256]{2,1,0:T(8,128)S(1)}, s32[16,128]{1,0:T(8,128)S(1)}, bf16[2,256,256]{2,1,0:T(8,128)(2,1)S(1)}, bf16[2,256,256]{2,1,0:T(8,128)(2,1)S(1)},...) custom-call(s32[1]{0:T(128)} %bitcast.me_ref, ...), custom_call_target="tpu_custom_call" | custom-call | flops 150994944 | bytes 6291456 | tf_op jit(solution)/shard_map/side/pallas_call | solution.py:489
  28.8 0.0 copy-start.11
  28.9 0.6 %copy-done.11 = f32[8,16,256]{2,1,0:T(8,128)} copy-done((f32[8,16,256]{2,1,0:T(8,128)}, f32[8,16,256]{2,1,0:T(8,128)S(1)}, u32[]{:S(2)}) %copy-start.11) | copy-done | bytes 131096
  29.5 0.0 all-to-all-done.group_ref
  29.5 0.3 middle.1
  29.8 3.5 %collective-permute-start = (f32[320,128]{1,0:T(8,128)S(1)}, f32[320,128]{1,0:T(8,128)S(1)}, u32[]{:S(2)}, u32[]{:S(2)}) collective-permute-start(f32[320,128]{1,0:T(8,128)S(1)} %get-tuple-element.25), channel_id=1, source_target_pairs={{0,8},{1,9},{2,10},{3,11},{8,16},{9,17},{10,18},{11,19},{12,4},{13... | collective-permute-start | bytes 491528 | tf_op jit(solution)/shard_map/ppermute | solution.py:527
  33.3 13.6 %all-gather = f32[32,8,128]{2,1,0:T(8,128)S(1)} all-gather(f32[8,8,128]{2,1,0:T(8,128)S(1)} %get-tuple-element.26), channel_id=2, replica_groups={{0,8,16,24},{1,9,17,25},{2,10,18,26},{3,11,19,27},{4,12,20,28},{5,13,21..., dimensions={0}, use_global_device_ids=true | all-gather | bytes 163840 | tf_op jit(solution)/shard_map/all_gather | solution.py:529
  46.9 0.0 collective-permute-done.half_ref
  46.9 0.0 copy-done.16
  46.9 0.0 copy-done.19
  46.9 0.0 copy-start.12
  46.9 0.9 %copy-done.12 = f32[8,16,256]{2,1,0:T(8,128)S(1)} copy-done((f32[8,16,256]{2,1,0:T(8,128)S(1)}, f32[8,16,256]{2,1,0:T(8,128)}, u32[]{:S(2)}) %copy-start.12) | copy-done | bytes 131096
  47.8 3.7 %down.1 = f32[16,2048]{1,0:T(8,128)} custom-call(s32[1]{0:T(128)} %bitcast.me_ref, f32[8,104,128]{2,1,0:T(8,128)S(1)} %all-to-all-done.group_ref, f32[320,128]{1,0:T(8,128)S(1)} %collective-permute-done.half_ref, f32[4,8,8,128]{3,2,1,0:T(8,128)S(1)} %bitcast.9, f32[8,16,256]{2,1,0:T(8,128)S(1)} %copy-done.12, s32[16,128]{1,0:T(8,128)S(1)} %get-tuple-element.28.inverse_ref, ...), custom_call_target="tpu_custom_call" | custom-call | tf_op jit(solution)/shard_map/down/pallas_call | solution.py:531
Async XLA Ops:
  0.0 1.0 %copy-start.1 = (f32[8,256,64]{1,2,0:T(8,128)S(1)}, f32[8,256,64]{1,2,0:T(8,128)}, u32[]{:S(2)}) copy-start(f32[8,256,64]{1,2,0:T(8,128)} %param.15) | copy-start | bytes 1572868
  1.0 0.9 %copy-start.4 = (f32[8,64,64]{2,1,0:T(8,128)S(1)}, f32[8,64,64]{2,1,0:T(8,128)}, u32[]{:S(2)}) copy-start(f32[8,64,64]{2,1,0:T(8,128)} %lift_hbm.3) | copy-start | bytes 393220
  2.0 0.9 %copy-start.10 = (f32[16,2048]{1,0:T(8,128)S(1)}, f32[16,2048]{1,0:T(8,128)}, u32[]{:S(2)}) copy-start(f32[16,2048]{1,0:T(8,128)} %points_hbm.1) | copy-start | bytes 393220
  2.9 0.7 %copy-start.14 = (s32[2048]{0:T(1024)S(1)}, s32[2048]{0:T(1024)}, u32[]{:S(2)}) copy-start(s32[2048]{0:T(1024)} %param.14) | copy-start | bytes 24580
  3.6 43.3 %copy-start.16 = (s32[8,8]{1,0:T(8,128)S(1)}, s32[8,8]{1,0:T(8,128)}, u32[]{:S(2)}) copy-start(s32[8,8]{1,0:T(8,128)} %far_ids_hbm.1) | copy-start | bytes 772
  3.6 43.3 %copy-start.19 = (s32[8]{0:T(128)S(1)}, s32[8]{0:T(128)}, u32[]{:S(2)}) copy-start(s32[8]{0:T(128)} %far_count_hbm.1) | copy-start | bytes 100
  5.9 0.7 %copy-start.8 = (f32[8,16,256]{2,1,0:T(8,128)}, f32[8,16,256]{2,1,0:T(8,128)S(1)}, u32[]{:S(2)}) copy-start(f32[8,16,256]{2,1,0:T(8,128)S(1)} %get-tuple-element.22.x_ref) | copy-start | bytes 393220
  6.6 22.9 %all-to-all-start = ((f32[8,104,128]{2,1,0:T(8,128)}), f32[8,104,128]{2,1,0:T(8,128)S(1)}, u32[]{:S(2)}, u32[]{:S(2)}) async-start(f32[8,104,128]{2,1,0:T(8,128)} %get-tuple-element.21), calls=%async_computation | async-start | bytes 851968 | tf_op jit(solution)/shard_map/all_to_all | solution.py:456
  11.7 2.8 %copy-start = (f32[8,3,256,256]{3,2,1,0:T(8,128)S(1)}, f32[8,3,256,256]{3,2,1,0:T(8,128)}, u32[]{:S(2)}) copy-start(f32[8,3,256,256]{3,2,1,0:T(8,128)} %blocks_hbm.1) | copy-start | bytes 18874372
  14.5 1.0 %copy-start.2 = (f32[8,256,64]{1,2,0:T(8,128)S(1)}, f32[8,256,64]{1,2,0:T(8,128)}, u32[]{:S(2)}) copy-start(f32[8,256,64]{1,2,0:T(8,128)} %param.15) | copy-start | bytes 1572868
  15.6 1.6 %copy-start.3 = (f32[8,8,64,64]{3,2,1,0:T(8,128)S(1)}, f32[8,8,64,64]{3,2,1,0:T(8,128)}, u32[]{:S(2)}) copy-start(f32[8,8,64,64]{3,2,1,0:T(8,128)} %far_hbm.1) | copy-start | bytes 3145732
  17.1 0.9 %copy-start.5 = (f32[8,64,64]{2,1,0:T(8,128)S(1)}, f32[8,64,64]{2,1,0:T(8,128)}, u32[]{:S(2)}) copy-start(f32[8,64,64]{2,1,0:T(8,128)} %lift_hbm.3) | copy-start | bytes 393220
  18.1 1.0 %copy-start.6 = (f32[4,4,64,64]{3,2,1,0:T(8,128)S(1)}, f32[4,4,64,64]{3,2,1,0:T(8,128)}, u32[]{:S(2)}) copy-start(f32[4,4,64,64]{3,2,1,0:T(8,128)} %couple_hbm.1) | copy-start | bytes 786436
  19.1 0.9 %copy-start.7 = (f32[4,2,64,64]{3,2,1,0:T(8,128)S(1)}, f32[4,2,64,64]{3,2,1,0:T(8,128)}, u32[]{:S(2)}) copy-start(f32[4,2,64,64]{3,2,1,0:T(8,128)} %transfer_hbm.1) | copy-start | bytes 393220
  20.1 0.9 %copy-start.9 = (f32[8,16,256]{2,1,0:T(8,128)S(1)}, f32[8,16,256]{2,1,0:T(8,128)}, u32[]{:S(2)}) copy-start(f32[8,16,256]{2,1,0:T(8,128)} %copy-done.8) | copy-start | bytes 393220
  21.0 0.8 %copy-start.13 = (f32[64,64]{1,0:T(8,128)S(1)}, f32[64,64]{1,0:T(8,128)}, u32[]{:S(2)}) copy-start(f32[64,64]{1,0:T(8,128)} %top_hbm.1) | copy-start | bytes 49156
  21.8 0.7 %copy-start.15 = (s32[2048]{0:T(1024)S(1)}, s32[2048]{0:T(1024)}, u32[]{:S(2)}) copy-start(s32[2048]{0:T(1024)} %param.14) | copy-start | bytes 24580
  22.4 0.7 %copy-start.17 = (s32[8,3]{0,1:T(4,128)S(1)}, s32[8,3]{0,1:T(4,128)}, u32[]{:S(2)}) copy-start(s32[8,3]{0,1:T(4,128)} %param.17) | copy-start | bytes 292
  23.1 0.7 %copy-start.18 = (s32[1,4,4]{2,1,0:T(4,128)S(1)}, s32[1,4,4]{2,1,0:T(4,128)}, u32[]{:S(2)}) copy-start(s32[1,4,4]{2,1,0:T(4,128)} %param.24) | copy-start | bytes 196
  28.8 0.7 %copy-start.11 = (f32[8,16,256]{2,1,0:T(8,128)}, f32[8,16,256]{2,1,0:T(8,128)S(1)}, u32[]{:S(2)}) copy-start(f32[8,16,256]{2,1,0:T(8,128)S(1)} %get-tuple-element.27.near_ref) | copy-start | bytes 393220
  29.8 17.1 %collective-permute-start = (f32[320,128]{1,0:T(8,128)S(1)}, f32[320,128]{1,0:T(8,128)S(1)}, u32[]{:S(2)}, u32[]{:S(2)}) collective-permute-start(f32[320,128]{1,0:T(8,128)S(1)} %get-tuple-element.25), channel_id=1, source_target_pairs={{0,8},{1,9},{2,10},{3,11},{8,16},{9,17},{10,18},{11,19},{12,4},{13... | collective-permute-start | bytes 491528 | tf_op jit(solution)/shard_map/ppermute | solution.py:527
  46.9 0.9 %copy-start.12 = (f32[8,16,256]{2,1,0:T(8,128)S(1)}, f32[8,16,256]{2,1,0:T(8,128)}, u32[]{:S(2)}) copy-start(f32[8,16,256]{2,1,0:T(8,128)} %copy-done.11) | copy-start | bytes 393220
